TPU v7x, 256 devices: a whole 4x4x8 slice. The times are simulated.
256 devices in a mesh: rep: 4 (over y_lo, core), fsdp: 64 (over x, z, y_hi).
Axes of the slice: x: 4, y: 4 (y_hi: 2, y_lo: 2; y = y_hi * 2 + y_lo), z: 8, core: 2. Of those that a mesh axis runs over, the one named last changes fastest.
Arguments:
- tokens: bfloat16 [4, 16384, 8192], P('rep', 'fsdp'), may hold values from -16 to 16
- weight: bfloat16 [4, 8192, 512], P('rep', 'fsdp'), may hold values from -6 to 6
- moment: bfloat16 [4, 8192, 512], P('rep', 'fsdp'), may hold values from -6 to 6
- second: bfloat16 [4, 8192, 512], P('rep', 'fsdp'), may hold values from 0.049804688 to 2
- cotangent: bfloat16 [4, 16384, 512], P('rep', 'fsdp'), may hold values from -12 to 12
- lengths: int32 [4, 4], P('rep'), may hold values from 2048 to 4096
- fragment: int32 [4], replicated, may hold values from 0 to 3, each once
- anchor: float32 [8192, 512], P('fsdp'), may hold values from -6 to 6
- velocity: float32 [8192, 512], P('fsdp'), may hold values from -4 to 4
- outer_grad: bfloat16 [4, 8192, 128], P('rep', 'fsdp'), may hold values from -4 to 4
Outputs:
- projected: bfloat16 [4, 16384, 512], P('rep', 'fsdp')
- input_grad: bfloat16 [4, 16384, 8192], P('rep', 'fsdp')
- weight_new: bfloat16 [4, 8192, 512], P('rep', 'fsdp')
- moment_new: bfloat16 [4, 8192, 512], P('rep', 'fsdp')
- second_new: bfloat16 [4, 8192, 512], P('rep', 'fsdp')
- anchor_new: float32 [8192, 128], P('fsdp')
- velocity_new: float32 [8192, 128], P('fsdp')
- drift: float32 [4, 8192, 512], P('rep', 'fsdp')
Inputs may be any that keep to these rules, and one draw needn't show every extreme that they name: fragment names each fragment index once.
All inputs are finite; a program needn't handle non-finite values.
Results may differ from a plain program's by a relative error of at most 0.0059.
Values may be sent and summed in bfloat16 or wider, within the bound.
No kernel may reach another device: no remote copies, remote signals or barrier semaphores. Data moves between devices by JAX's collectives and lax.ppermute only.
A program may use at most 128 MiB of HBM per device.

v0:
```python
import math

import jax
import jax.numpy as jnp
from jax import lax
from jax.sharding import PartitionSpec as P

D = 8192
HEAD = 128


def contract_rows(left, right):
    return lax.dot_general(
        left, right, (((0,), (0,)), ((), ())), preferred_element_type=jnp.float32
    )


def per_device(
    tokens, weight, moment, second, cotangent, lengths, fragment, anchor, velocity, outer_grad
):
    scale = 1.0 / math.sqrt(D)
    local_x = tokens[0]
    local_w = weight[0]
    tok_count = local_x.shape[0]
    whole_w = lax.all_gather(local_w, "fsdp", axis=0, tiled=True)
    projected = (jnp.dot(local_x, whole_w, preferred_element_type=jnp.float32) * scale).astype(
        jnp.bfloat16
    )
    total_tokens = tok_count * lax.axis_size("fsdp")
    seq_count = lengths.shape[1]
    seq_len = total_tokens // seq_count
    positions = lax.axis_index("fsdp") * tok_count + jnp.arange(tok_count, dtype=jnp.int32)
    sequence = positions // seq_len
    offset = positions % seq_len
    picks = (sequence[:, None] == jnp.arange(seq_count, dtype=jnp.int32)[None, :]).astype(jnp.int32)
    limit = jnp.sum(picks * lengths[0][None, :], axis=1)
    live = (offset < limit).astype(jnp.float32)
    masked = (cotangent[0].astype(jnp.float32) * live[:, None]).astype(jnp.bfloat16)
    input_grad = lax.dot_general(
        masked, whole_w, (((1,), (1,)), ((), ())), preferred_element_type=jnp.float32
    )
    input_grad = (input_grad * scale).astype(jnp.bfloat16)
    grad = lax.psum_scatter(
        contract_rows(local_x, masked) * scale, "fsdp", scatter_dimension=0, tiled=True
    )
    first = 0.9 * moment[0].astype(jnp.float32) + 0.1 * grad
    sec = 0.95 * second[0].astype(jnp.float32) + 0.05 * grad * grad
    old = local_w.astype(jnp.float32)
    stepped = old - 0.01 * (first / (jnp.sqrt(sec) + 1e-08) + 0.1 * old)
    blocks = []
    for order in range(fragment.shape[0]):
        begin_col = fragment[order] * HEAD
        blocks.append(
            lax.dynamic_slice_in_dim(anchor, begin_col, HEAD, 1)
            - lax.dynamic_slice_in_dim(stepped, begin_col, HEAD, 1)
        )
    drift = jnp.concatenate(blocks, axis=1)
    start_col = fragment[0] * HEAD
    vel_cols = lax.dynamic_slice_in_dim(velocity, start_col, HEAD, 1)
    anc_cols = lax.dynamic_slice_in_dim(anchor, start_col, HEAD, 1)
    replicas = lax.axis_size("rep")
    outer_local = outer_grad[0].astype(jnp.float32)
    outer_mean = lax.psum(outer_local.astype(jnp.bfloat16), "rep").astype(jnp.float32) / replicas
    velocity_new = 0.9 * vel_cols + outer_mean
    anchor_new = anc_cols - 0.7 * (outer_mean + 0.9 * velocity_new)
    mixed = 0.5 * lax.dynamic_slice_in_dim(stepped, start_col, HEAD, 1) + 0.5 * anchor_new
    stepped = lax.dynamic_update_slice_in_dim(stepped, mixed, start_col, 1)
    return (
        projected[None],
        input_grad[None],
        stepped.astype(jnp.bfloat16)[None],
        first.astype(jnp.bfloat16)[None],
        sec.astype(jnp.bfloat16)[None],
        anchor_new,
        velocity_new,
        drift[None],
    )


def solution(mesh):
    return jax.shard_map(
        per_device,
        mesh=mesh,
        in_specs=(
            P("rep", "fsdp", None),
            P("rep", "fsdp", None),
            P("rep", "fsdp", None),
            P("rep", "fsdp", None),
            P("rep", "fsdp", None),
            P("rep", None),
            P(),
            P("fsdp", None),
            P("fsdp", None),
            P("rep", "fsdp", None),
        ),
        out_specs=(
            P("rep", "fsdp", None),
            P("rep", "fsdp", None),
            P("rep", "fsdp", None),
            P("rep", "fsdp", None),
            P("rep", "fsdp", None),
            P("fsdp", None),
            P("fsdp", None),
            P("rep", "fsdp", None),
        ),
        check_vma=False,
    )
```

profile of v0, /device:TPU:8, one launch (start us, length us, event | category | flops | bytes accessed | tf_op | source)
XLA Modules:
  0.0 573.9 jit_solution(18250368415455537299)
XLA Ops:
  7.2 0.0 copy-start
  7.2 0.0 all-gather.3.cloned.1.call-start
  7.2 0.7 all-gather.3.cloned.1.call-update
  7.9 0.0 reduce-scatter.2.cloned.1.call-start
  8.0 0.7 select_reduce_fusion
  8.7 10.5 %multiply_bitcast_fusion = f32[8192,512]{0,1:T(8,128)} fusion(bf16[1,256,8192]{2,1,0:T(8,128)(2,1)} %param.10, bf16[1,256,512]{2,1,0:T(8,128)(2,1)} %param.14, f32[256]{0:T(256)S(1)} %compare_convert_fusion), kind=kOutput, calls=%fused_computation | convolution fusion | flops 2152071168 | bytes 21234688 | tf_op jit(solution)/shard_map/dot_general | solution.py:13
  19.2 0.0 copy-start.7
  19.3 0.0 reduce-scatter.2.cloned.1.call-update
  19.3 0.6 copy-done.9
  19.9 0.6 fusion.38
  23.1 0.1 copy.33
  23.3 0.1 copy.48
  23.4 0.1 copy.50
  23.5 0.1 copy.51
  23.6 0.1 copy.52
  23.7 0.1 copy.49
  23.8 0.1 copy.34
  24.0 0.1 copy.35
  24.1 0.1 copy.37
  24.2 10.7 %psum.7 = bf16[128,128]{0,1:T(8,128)(2,1)S(1)} all-reduce(bf16[128,128]{0,1:T(8,128)(2,1)S(1)} %bitcast.71), channel_id=1, replica_groups=mesh['rep'=4,'fsdp'=64] {'rep'}, use_global_device_ids=true, to_apply=%region_2.3 | all-reduce | flops 16384 | bytes 65536 | tf_op jit(solution)/shard_map/psum | solution.py:63
  34.9 125.7 %all-gather.3.cloned.1.call-done = bf16[1,8192,512]{2,1,0:T(8,128)(2,1)} async-done(((bf16[1,128,512]{2,1,0:T(8,128)(2,1)}), bf16[1,8192,512]{2,1,0:T(8,128)(2,1)}) %all-gather.3.cloned.1.call-update) | async-done | bytes 8388624 | tf_op jit(solution)/shard_map/all_gather | solution.py:25
  160.6 7.9 %fusion.1 = bf16[1,256,8192]{2,1,0:T(8,128)(2,1)} fusion(bf16[1,8192,512]{2,1,0:T(8,128)(2,1)} %all-gather.3.cloned.1.call-done, bf16[1,256,512]{2,1,0:T(8,128)(2,1)S(1)} %copy-done.3, f32[256]{0:T(256)S(1)} %compare_convert_fusion), kind=kOutput, calls=%fused_computation.3 | convolution fusion | flops 2152071168 | bytes 12846080 | tf_op jit(solution)/shard_map/dot_general | solution.py:39
  168.6 3.0 fusion.17
  171.6 389.6 %reduce-scatter.2.cloned.1.call-done = f32[128,512]{0,1:T(8,128)} async-done(((f32[8192,512]{0,1:T(8,128)}), f32[128,512]{0,1:T(8,128)}) %reduce-scatter.2.cloned.1.call-update) | async-done | bytes 262160 | tf_op jit(solution)/shard_map/reduce_scatter | solution.py:43
  561.2 1.2 fusion.35
  562.4 0.1 dynamic-slice_subtract_fusion.2
  562.5 0.8 copy.47
  563.3 0.8 copy.42
  564.1 0.7 copy.45
  564.8 0.7 copy.46
  565.5 0.8 copy.43
  566.3 0.8 copy.44
  (22 shorter events, 0.2 us)
Async XLA Ops:
  7.2 16.5 %copy-start = (f32[128,512]{1,0:T(8,128)S(1)}, f32[128,512]{1,0:T(8,128)}, u32[]{:S(2)}) copy-start(f32[128,512]{1,0:T(8,128)} %param.18) | copy-start | bytes 786436
  7.2 153.4 %all-gather.3.cloned.1.call-start = ((), (), s32[]{:S(2)}) async-start(), calls=%async_computation.2 | async-start | bytes 8519680 | tf_op jit(solution)/shard_map/all_gather | solution.py:25
  7.9 553.3 %reduce-scatter.2.cloned.1.call-start = ((), (), s32[]{:S(2)}) async-start(), calls=%async_computation.1 | async-start | bytes 17039360 | tf_op jit(solution)/shard_map/reduce_scatter | solution.py:43
  19.2 0.7 copy-start.9
  19.2 3.9 copy-start.4
  19.2 4.0 copy-start.5
  19.2 4.6 copy-start.6
  19.2 4.7 copy-start.7
  19.3 4.8 copy-start.8
  19.3 141.4 %copy-start.3 = (bf16[1,256,512]{2,1,0:T(8,128)(2,1)S(1)}, bf16[1,256,512]{2,1,0:T(8,128)(2,1)}, u32[]{:S(2)}) copy-start(bf16[1,256,512]{2,1,0:T(8,128)(2,1)} %param.14) | copy-start | bytes 786436
  160.6 7.9 %copy-start.1 = (bf16[1,8192,512]{2,1,0:T(8,128)(2,1)S(1)}, bf16[1,8192,512]{2,1,0:T(8,128)(2,1)}, u32[]{:S(2)}) copy-start(bf16[1,8192,512]{2,1,0:T(8,128)(2,1)} %all-gather.3.cloned.1.call-done) | copy-start | bytes 25165828
  160.6 7.9 %copy-start.2 = (bf16[1,256,8192]{2,1,0:T(8,128)(2,1)S(1)}, bf16[1,256,8192]{2,1,0:T(8,128)(2,1)}, u32[]{:S(2)}) copy-start(bf16[1,256,8192]{2,1,0:T(8,128)(2,1)} %param.10) | copy-start | bytes 12582916
Sparse Core Ops, SparseCore 0:
  11.6 148.9 all-gather.2
  163.2 397.9 reduce-scatter.1
where the time goes:
time: 574 us
  waiting for transfers between devices  516 us (90%)
  matrix products  21.5 us (4%)
  between operations  16.9 us (3%)
  blocking collectives  10.7 us (2%)
  local copies, waits for them, and re-layouts  6.8 us (1%)
    reduce_scatter x1, waiting for transfers between devices, per_device(): lax.psum_scatter(contract_rows(local_x, masked) * scale, 'fsdp', scatter_...  390 us
    all_gather x1, waiting for transfers between devices, per_device(): whole_w = lax.all_gather(local_w, 'fsdp', axis=0, tiled=True)  126 us
  transfers between devices with their start and end apart: 2, of which 2 were waited for; matrix products, arithmetic and copies ran while one was open for 4% of the time, Pallas kernels for 0%

commit v1 on v0

v1 whole, which is shorter than its diff:
```python
import functools
import math

import jax
import jax.numpy as jnp
from jax import lax
from jax.experimental import pallas as pl
from jax.experimental.pallas import tpu as pltpu
from jax.sharding import PartitionSpec as P

D = 8192
KV = 512
HEAD = 128
NX, NZ, NY = 4, 8, 2
SLOT = D // (NX * NZ)
ROWS = SLOT // NY
PART = KV // 2
LOAD = 3 * D // (2 * NZ)
SCALE = 1.0 / math.sqrt(D)
AXES = ("rep", "fsdp")
BF = jnp.bfloat16
F32 = jnp.float32


def device_index(x, z, y, core):
    y_hi, y_lo = y // 2, y % 2
    return (y_lo * 2 + core) * 64 + (x * NZ + z) * NY + y_hi


def moved(value, dx=0, dz=0, dy=0, dcore=0):
    pairs = []
    for x in range(NX):
        for z in range(NZ):
            for y in range(4):
                for core in range(2):
                    source = device_index(x, z, y, core)
                    target = device_index(
                        (x + dx) % NX, (z + dz) % NZ, (y + dy) % 4, (core + dcore) % 2
                    )
                    pairs.append((source, target))
    return lax.ppermute(value, AXES, sorted(pairs))


def swap_y_lo(value):
    pairs = []
    for rep in range(4):
        for place in range(64):
            pairs.append((rep * 64 + place, (rep ^ 2) * 64 + place))
    return lax.ppermute(value, AXES, pairs)


def together(*values):
    return lax.optimization_barrier(values)


def both_ways(to_right, to_left, axis):
    to_right, to_left = together(to_right, to_left)
    return together(moved(to_right, **{axis: 1}), moved(to_left, **{axis: -1}))


def contract(left, right, left_dim, right_dim):
    return lax.dot_general(
        left, right, (((left_dim,), (right_dim,)), ((), ())), preferred_element_type=F32
    )


def call(
    kernel, grid, scalars, ins, outs, flops, moved_bytes, scratch=(), aliases=None, limit=20
):
    shapes = [jax.ShapeDtypeStruct(shape, kind) for shape, kind, _ in outs]
    return pl.pallas_call(
        kernel,
        out_shape=shapes,
        grid_spec=pltpu.PrefetchScalarGridSpec(
            num_scalar_prefetch=1,
            grid=grid,
            in_specs=[spec for _, spec in ins],
            out_specs=[spec for _, _, spec in outs],
            scratch_shapes=list(scratch),
        ),
        input_output_aliases=aliases or {},
        compiler_params=pltpu.CompilerParams(vmem_limit_bytes=limit << 20),
        cost_estimate=pl.CostEstimate(
            flops=flops, bytes_accessed=moved_bytes, transcendentals=0
        ),
    )(scalars, *[value for value, _ in ins])


def whole(*shape):
    return pl.BlockSpec(shape, lambda *_: (0,) * len(shape))


def live_rows(cotangent, at):
    row = lax.broadcasted_iota(jnp.int32, cotangent.shape, 0)
    return jnp.where(row < at[3], cotangent, jnp.zeros_like(cotangent))


def token_specs(count, shift, y=None):
    def spec(col):
        if y is None:
            return pl.BlockSpec((count, SLOT), lambda i, at: (0, col * NZ + lax.rem(at[1] + shift, NZ)))

        def place(i, at):
            z = lax.rem(at[1] + (shift(i) if callable(shift) else shift), NZ)
            return 0, (col * NZ + z) * NY + (at[2] if y == 0 else 1 - at[2])

        return pl.BlockSpec((count, ROWS), place)

    return [spec(col) for col in range(NX)]


def joined(refs):
    return jnp.concatenate([ref[...] for ref in refs], axis=1)


def first_kernel(at, *refs):
    toks, (cotangent, rows, out) = refs[:NX], refs[NX:]
    rows[...] = live_rows(cotangent[...], at).T
    out[0] = contract(rows[PART:], joined(toks), 1, 0).astype(BF)


def first_block(tokens, cotangent, at):
    count = tokens.shape[0]
    ins = [(tokens, spec) for spec in token_specs(count, lambda i: NZ // 2, 1)]
    ins += [(cotangent, whole(count, KV))]
    outs = [((KV, count), BF, whole(KV, count))]
    outs += [((1, PART, NX * ROWS), BF, whole(1, PART, NX * ROWS))]
    return call(first_kernel, (1,), at, ins, outs, PART * count * NX * SLOT, 1 << 20)


def twin_kernel(at, *refs):
    toks, rows, out = refs[:NX], *refs[NX:]
    out[0] = contract(rows[...], joined(toks), 1, 0).astype(BF)


def twin_blocks(tokens, rows, at, steps):
    count = tokens.shape[0]

    def shift(i):
        value = steps[-1] % NZ
        for order in range(len(steps) - 2, -1, -1):
            value = jnp.where(i == order, steps[order] % NZ, value)
        return value

    ins = [(tokens, spec) for spec in token_specs(count, shift, 1)] + [(rows, whole(PART, count))]
    block = pl.BlockSpec((1, PART, NX * ROWS), lambda i, at: (i, 0, 0))
    outs = [((len(steps), PART, NX * ROWS), BF, block)]
    flops = 2 * PART * count * NX * ROWS * len(steps)
    return call(twin_kernel, (len(steps),), at, ins, outs, flops, len(steps) << 19)[0]


def terms(toks, rows, y_hi):
    wide = [contract(rows[:PART], tok[...], 1, 0) for tok in toks]
    begin = pl.multiple_of(y_hi * ROWS, ROWS)
    narrow = jnp.concatenate([tok[:, pl.ds(begin, ROWS)] for tok in toks], axis=1)
    return wide + [contract(rows[PART:], narrow, 1, 0)]


def far_kernel(at, *refs):
    toks, (rows, came, out_r, out_l) = refs[:NX], refs[NX:]
    parts = terms(toks, rows, at[2])
    parts[NX] = parts[NX] + came[0].astype(F32)
    value = jnp.concatenate(parts, axis=1).astype(BF)
    out_r[...] = value[: PART // 2]
    out_l[...] = value[PART // 2 :]


def far_block(tokens, rows, came, at):
    count = tokens.shape[0]
    ins = [(tokens, spec) for spec in token_specs(count, 4)]
    ins += [(rows, whole(KV, count)), (came, whole(1, PART, NX * ROWS))]
    outs = [((PART // 2, LOAD), BF, whole(PART // 2, LOAD))] * 2
    return call(far_kernel, (1,), at, ins, outs, 2 * PART * count * LOAD, 3 << 19)


def step_kernel(upper, at, *refs):
    toks, (rows, came, moving, out) = refs[:NX], refs[NX:]
    parts = terms(toks, rows, at[2])
    parts[NX] = parts[NX] + came[0].astype(F32)
    size = moving.shape[0]
    begin = PART - size if upper else 0
    col = 0
    for part in parts:
        cols = slice(col, col + part.shape[1])
        col += part.shape[1]
        rows_in = slice(begin, begin + size)
        out[rows_in, cols] = (part[rows_in] + moving[:, cols].astype(F32)).astype(BF)
        if size < PART:
            rest = slice(0, begin) if upper else slice(size, PART)
            out[rest, cols] = part[rest].astype(BF)


def step_block(tokens, rows, came, order, moving, at, step):
    count = tokens.shape[0]
    ins = [(tokens, spec) for spec in token_specs(count, step % NZ)]
    ins += [
        (rows, whole(KV, count)),
        (came, pl.BlockSpec((1, PART, NX * ROWS), lambda i, at: (order, 0, 0))),
        (moving, whole(*moving.shape)),
    ]
    outs = [((PART, LOAD), BF, whole(PART, LOAD))]
    kernel = functools.partial(step_kernel, step < 0)
    return call(kernel, (1,), at, ins, outs, 2 * PART * count * LOAD, 5 << 19)[0]


def last_kernel(at, tok, rows, came, *refs):
    moving_p, moving_q, (own, out_1, out_2, out_3) = refs[:2], refs[2:4], refs[4:]
    i = pl.program_id(0)
    wide, narrow = terms([tok], rows, at[2])
    wide = wide + (moving_p[0][...].astype(F32) + moving_p[1][...].astype(F32))
    narrow = narrow + came[0].astype(F32)
    narrow = narrow + (moving_q[0][...].astype(F32) + moving_q[1][...].astype(F32))
    for step, out in ((0, own), (1, out_1), (2, out_2), (3, out_3)):

        @pl.when(i == step)
        def _(out=out):
            out[:, :SLOT] = wide.astype(out.dtype)
            out[:, SLOT:] = narrow.astype(out.dtype)


def last_block(tokens, rows, came, order, right, left, at):
    count = tokens.shape[0]

    def column(i, at):
        return lax.rem(at[0] + i, NX)

    tok = pl.BlockSpec((count, SLOT), lambda i, at: (0, column(i, at) * NZ + at[1]))
    wide = pl.BlockSpec((PART, SLOT), lambda i, at: (0, column(i, at)))
    narrow = pl.BlockSpec((PART, ROWS), lambda i, at: (0, NX * NY + column(i, at)))
    twin = pl.BlockSpec((1, PART, ROWS), lambda i, at: (order, 0, column(i, at)))
    ins = [(tokens, tok), (rows, whole(KV, count)), (came, twin)]
    ins += [(right, wide), (left, wide), (right, narrow), (left, narrow)]
    size = SLOT + ROWS
    outs = [((PART, size), F32, whole(PART, size))]
    outs += [((PART, size), BF, whole(PART, size))] * 3
    return call(last_kernel, (NX,), at, ins, outs, 2 * PART * count * LOAD, 4 << 20)


def split_kernel(at, own, in_1, in_2, in_3, keep, send):
    value = own[...] + (
        in_1[...].astype(F32) + in_2[...].astype(F32) + in_3[...].astype(F32)
    )
    keep[PART:] = value[:, SLOT:]
    for y in range(NY):

        @pl.when(at[2] == y)
        def _(y=y):
            keep[:PART] = value[:, y * ROWS : (y + 1) * ROWS]
            send[...] = value[:, (1 - y) * ROWS : (2 - y) * ROWS].astype(BF)


def split_y(own, came, at):
    full = whole(PART, SLOT + ROWS)
    ins = [(own, full)] + [(value, full) for value in came]
    outs = [((KV, ROWS), F32, whole(KV, ROWS)), ((PART, ROWS), BF, whole(PART, ROWS))]
    return call(split_kernel, (1,), at, ins, outs, 1 << 20, 3 << 19)


def spread_x(pieces):
    pieces = together(*pieces)
    return together(*[moved(value, dx=step) for step, value in zip((1, 2, 3), pieces)])


def weight_kernel(first, last, at, tok, cotangent, near, twin, *rest):
    sums, (out, grad, both) = (None if first else rest[0]), rest[-3:]
    z, y_hi = at[1], at[2]
    for order in range(NZ):
        slot = lax.rem(z + order, NZ) * SLOT
        low = pl.multiple_of(slot + y_hi * ROWS, ROWS)
        high = pl.multiple_of(slot + (1 - y_hi) * ROWS, ROWS)
        both[pl.ds(low, ROWS)] = near[order * ROWS : (order + 1) * ROWS]
        both[pl.ds(high, ROWS)] = twin[order * ROWS : (order + 1) * ROWS]
    part = contract(tok[...], both[...], 1, 0)
    if not first:
        part = part + sums[...]
    out[...] = (part * SCALE).astype(BF) if last else part
    masked = live_rows(cotangent[...], at)
    grad[...] = (contract(masked, both[...], 1, 1) * SCALE).astype(BF)


def use_weight(tokens, cotangent, pair, state, at, step, last):
    count = tokens.shape[0]
    first = state is None
    width = NZ * SLOT
    wide = pl.BlockSpec((count, width), lambda i, at: (0, lax.rem(at[0] + step, NX)))
    block = whole(NZ * ROWS, KV)
    ins = [(tokens, wide), (cotangent, whole(count, KV)), (pair[0], block), (pair[1], block)]
    aliases = None
    if not first:
        ins += [(state[0], whole(count, KV)), (state[1], pl.BlockSpec(memory_space=pl.ANY))]
        aliases = {len(ins): 1}
    outs = [((count, KV), BF if last else F32, whole(count, KV)), ((count, D), BF, wide)]
    kernel = functools.partial(weight_kernel, first, last)
    flops = 4 * count * KV * width
    return call(kernel, (1,), at, ins, outs, flops, 6 << 20, [pltpu.VMEM((width, KV), BF)], aliases)


def exchange(tokens, cotangent, local_w, at):
    rows, send = first_block(tokens, cotangent, at)
    rows_q = rows[PART:]
    local_w, send = together(local_w, send)
    twin_1 = moved(send, dy=2)
    low, high = [moved(local_w, dz=1)], [moved(local_w, dz=-1)]
    low[0], high[0], twin_1 = together(low[0], high[0], twin_1)

    low.append(moved(low[0], dz=1))
    high.append(moved(high[0], dz=-1))
    send = twin_blocks(tokens, rows_q, at, (3, -3))
    right, left = far_block(tokens, rows, twin_1, at)
    low[1], high[1], right, left, send = together(low[1], high[1], right, left, send)

    right, left = moved(right, dz=1), moved(left, dz=-1)
    low.append(moved(low[1], dz=1))
    high.append(moved(high[1], dz=-1))
    twin_2 = moved(send, dy=2)
    send = twin_blocks(tokens, rows_q, at, (2, -2))
    low[2], high[2], send = together(low[2], high[2], send)
    half = ROWS // 2
    far = moved(low[2][:half], dz=1), moved(high[2][half:], dz=-1)

    right = step_block(tokens, rows, twin_2, 0, right, at, 3)
    right, left = together(right, left)
    left = step_block(tokens, rows, twin_2, 1, left, at, -3)
    right, left, send, *far = together(right, left, send, *far)
    right, left = moved(right, dz=1), moved(left, dz=-1)
    twin_3 = moved(send, dy=2)
    near = jnp.concatenate([local_w] + high + list(far) + low[::-1], axis=0)
    send = twin_blocks(tokens, rows_q, at, (1, -1, 0))
    near, send = together(near, send)
    near_low, near_high = moved(near, dx=1), moved(near, dx=-1)
    twin = moved(near, dy=2)
    twin_4 = moved(send, dy=2)

    right = step_block(tokens, rows, twin_3, 0, right, at, 2)
    right, left = together(right, left)
    left = step_block(tokens, rows, twin_3, 1, left, at, -2)
    right, left = together(right, left)
    right, left = moved(right, dz=1), moved(left, dz=-1)
    near_low, near_high, twin = together(near_low, near_high, twin)
    twin_low, twin_high = moved(twin, dx=1), moved(twin, dx=-1)
    state = use_weight(tokens, cotangent, (near, twin), None, at, 0, False)

    right = step_block(tokens, rows, twin_4, 0, right, at, 1)
    right, left = together(right, left)
    left = step_block(tokens, rows, twin_4, 1, left, at, -1)
    right, left, *state = together(right, left, *state)
    right, left = moved(right, dz=1), moved(left, dz=-1)
    twin_low, twin_high = together(twin_low, twin_high)
    near_far, twin_far = moved(near_low, dx=1), moved(twin_high, dx=-1)
    state = use_weight(tokens, cotangent, (near_high, twin_high), state, at, 1, False)
    state = use_weight(tokens, cotangent, (near_low, twin_low), state, at, 3, False)
    right, left, *state = together(right, left, *state)

    own, *pieces = last_block(tokens, rows, twin_4, 2, right, left, at)
    came = spread_x(pieces)
    keep, send = split_y(own, came, at)
    came = moved(send, dy=2)
    state = use_weight(tokens, cotangent, (near_far, twin_far), state, at, 2, True)
    return state, (keep, came)


def update_kernel(
    frag, keep, came, weight, moment, second, anchor, velocity, two, far,
    weight_out, moment_out, second_out, anchor_out, velocity_out, drift_out, stepped,
):
    low = keep[:PART] + came[...].astype(F32)
    grad = jnp.concatenate([low, keep[PART:]], axis=0).T * SCALE
    first = 0.9 * moment[0].astype(F32) + 0.1 * grad
    sec = 0.95 * second[0].astype(F32) + 0.05 * grad * grad
    old = weight[0].astype(F32)
    value = old - 0.01 * (first / (jnp.sqrt(sec) + 1e-08) + 0.1 * old)
    moment_out[0] = first.astype(BF)
    second_out[0] = sec.astype(BF)
    weight_out[0] = value.astype(BF)
    stepped[...] = value

    def columns(order):
        return pl.ds(pl.multiple_of(frag[order] * HEAD, HEAD), HEAD)

    for order in range(KV // HEAD):
        cols = columns(order)
        drift_out[0, :, order * HEAD : (order + 1) * HEAD] = anchor[:, cols] - stepped[:, cols]
    cols = columns(0)
    mean = two[0].astype(F32) + two[1].astype(F32) + far[0].astype(F32) + far[1].astype(F32)
    mean = mean * 0.25
    velocity_new = 0.9 * velocity[:, cols] + mean
    anchor_new = anchor[:, cols] - 0.7 * (mean + 0.9 * velocity_new)
    velocity_out[...] = velocity_new
    anchor_out[...] = anchor_new
    weight_out[0, :, cols] = (0.5 * stepped[:, cols] + 0.5 * anchor_new).astype(BF)


def update(fragment, parts, weight, moment, second, anchor, velocity, two, far):
    values = (*parts, weight, moment, second, anchor, velocity, two, far)
    ins = [(value, whole(*value.shape)) for value in values]
    wide, narrow = (1, ROWS, KV), (ROWS, HEAD)
    kinds = [(wide, BF), (wide, BF), (wide, BF), (narrow, F32), (narrow, F32), (wide, F32)]
    outs = [(shape, kind, whole(*shape)) for shape, kind in kinds]
    scratch = [pltpu.VMEM((ROWS, KV), F32)]
    return call(update_kernel, (1,), fragment, ins, outs, 2 << 20, 3 << 20, scratch)


def per_device(
    tokens, weight, moment, second, cotangent, lengths, fragment, anchor, velocity, outer_grad
):
    place = lax.axis_index("fsdp")
    x, z, y_hi = place // (NZ * NY), (place // NY) % NZ, place % NY
    local_x, local_c = tokens[0], cotangent[0]
    tok_count = local_x.shape[0]

    seq_count = lengths.shape[1]
    holders = NX * NZ * NY // seq_count
    limit = lax.dynamic_index_in_dim(lengths[0], place // holders, keepdims=False)
    live = limit - (place % holders) * tok_count
    at = jnp.stack([x, z, y_hi, live]).astype(jnp.int32)

    (projected, input_grad), parts = exchange(local_x, local_c, weight[0], at)

    outer_own = outer_grad[0]
    outer_two = jnp.stack([outer_own, moved(outer_own, dcore=1)])
    outer_far = swap_y_lo(outer_two)

    weight_new, moment_new, second_new, anchor_new, velocity_new, drift = update(
        fragment, parts, weight, moment, second, anchor, velocity, outer_two, outer_far
    )
    return (
        projected[None],
        input_grad[None],
        weight_new,
        moment_new,
        second_new,
        anchor_new,
        velocity_new,
        drift,
    )


def solution(mesh):
    wide = P("rep", "fsdp", None)
    return jax.shard_map(
        per_device,
        mesh=mesh,
        in_specs=(
            wide,
            wide,
            wide,
            wide,
            wide,
            P("rep", None),
            P(),
            P("fsdp", None),
            P("fsdp", None),
            wide,
        ),
        out_specs=(
            wide,
            wide,
            wide,
            wide,
            wide,
            P("fsdp", None),
            P("fsdp", None),
            wide,
        ),
        check_vma=False,
    )
```

time: 574 us -> 151 us (0.26)
  waiting for transfers between devices: 516 us -> 59.1 us
  starting transfers between devices: 0.08 us -> 55.6 us
  Pallas kernels: 0 us -> 28.6 us
  matrix products: 21.5 us -> 0 us
  between operations: 16.9 us -> 1.64 us
  blocking collectives: 10.7 us -> 0 us
    reduce_scatter x1 -> x0, waiting for transfers between devices: 390 us -> none  [per_device(): lax.psum_scatter(contract_rows(local_x, masked) * scale, 'fsdp', scatter_...]
    all_gather x1 -> x0, waiting for transfers between devices: 126 us -> none  [per_device(): whole_w = lax.all_gather(local_w, 'fsdp', axis=0, tiled=True)]
    ppermute x0 -> x33, waiting for transfers between devices: none -> 59.1 us  [the longest x32 58.6 us: moved(): return lax.ppermute(value, AXES, sorted(pairs))]
    ppermute x0 -> x33, starting transfers between devices: none -> 55.6 us  [the longest x32 55.3 us: moved(): return lax.ppermute(value, AXES, sorted(pairs))]
    pallas_call x0 -> x18, Pallas kernels: none -> 28.6 us  [call(): pl.pallas_call(kernel, out_shape=shapes, grid_spec=pltpu.PrefetchScalarGr...]
    dot_general x3 -> x0, matrix products: 21.5 us -> none  [the longest x1 10.5 us: contract_rows(): lax.dot_general(left, right, (((0,), (0,)), ((), ())), preferred_element_...]
    psum x1 -> x0, blocking collectives: 10.7 us -> none  [per_device(): lax.psum(outer_local.astype(jnp.bfloat16), 'rep').astype(jnp.float32)]
  transfers between devices with their start and end apart: 2 -> 33, of which waited for: 2 -> 14; matrix products, arithmetic and copies ran while one was open for 4% -> 0% of each run, Pallas kernels for 0% -> 17%
where the time goes in v1:
time: 151 us; the launch traced here: 149 us
  waiting for transfers between devices  59.1 us (39%)
  starting transfers between devices  55.6 us (37%)
  Pallas kernels  28.6 us (19%)
  local copies, waits for them, and re-layouts  4.47 us (3%)
  between operations  1.64 us (1%)
    ppermute x32, waiting for transfers between devices, moved(): return lax.ppermute(value, AXES, sorted(pairs))  58.6 us
    ppermute x32, starting transfers between devices, moved(): return lax.ppermute(value, AXES, sorted(pairs))  55.3 us
    pallas_call x18, Pallas kernels, call(): pl.pallas_call(kernel, out_shape=shapes, grid_spec=pltpu.PrefetchScalarGr...  28.6 us
    unnamed x32, local copies, waits for them, and re-layouts  3.86 us
  transfers between devices with their start and end apart: 33, of which 14 were waited for; matrix products, arithmetic and copies ran while one was open for 0% of the time, Pallas kernels for 17%

profile of v1, /device:TPU:8, one launch (start us, length us, event | category | flops | bytes accessed | tf_op | source)
XLA Modules:
  0.0 149.5 jit_solution(87940637650521113)
XLA Ops:
  2.6 2.2 %copy-done.1 = bf16[1,256,8192]{2,1,0:T(8,128)(2,1)S(1)} copy-done((bf16[1,256,8192]{2,1,0:T(8,128)(2,1)S(1)}, bf16[1,256,8192]{2,1,0:T(8,128)(2,1)}, u32[]{:S(2)}) %copy-start.1) | copy-done | bytes 4194328
  6.6 2.4 %collective-permute-start.2 = (bf16[1,256,512]{2,1,0:T(8,128)(2,1)S(1)}, bf16[1,256,512]{2,1,0:T(8,128)(2,1)S(1)}, u32[]{:S(2)}, u32[]{:S(2)}) collective-permute-start(bf16[1,256,512]{2,1,0:T(8,128)(2,1)S(1)} %get-tuple-element.81), channel_id=1, source_target_pairs={{0,1},{1,0},{2,3},{3,2},{4,5},{5,4},{6,7},{7,6},{8,9},{9,8},{10,11... | collective-permute-start | bytes 786440 | tf_op jit(solution)/shard_map/ppermute | solution.py:41
  9.0 1.9 %collective-permute-start = (bf16[128,512]{1,0:T(8,128)(2,1)S(1)}, bf16[128,512]{1,0:T(8,128)(2,1)S(1)}, u32[]{:S(2)}, u32[]{:S(2)}) collective-permute-start(bf16[128,512]{1,0:T(8,128)(2,1)S(1)} %bitcast.66), channel_id=1, source_target_pairs={{0,2},{1,3},{2,4},{3,5},{4,6},{5,7},{6,8},{7,9},{8,10},{9,11},{10,... | collective-permute-start | bytes 393224 | tf_op jit(solution)/shard_map/ppermute | solution.py:41
  10.9 3.9 %collective-permute-start.1 = (bf16[128,512]{1,0:T(8,128)(2,1)S(1)}, bf16[128,512]{1,0:T(8,128)(2,1)S(1)}, u32[]{:S(2)}, u32[]{:S(2)}) collective-permute-start(bf16[128,512]{1,0:T(8,128)(2,1)S(1)} %bitcast.67), channel_id=1, source_target_pairs={{0,14},{1,15},{2,0},{3,1},{4,2},{5,3},{6,4},{7,5},{8,6},{9,7},{10,... | collective-permute-start | bytes 393224 | tf_op jit(solution)/shard_map/ppermute | solution.py:41
  14.9 3.2 %collective-permute-done = bf16[128,512]{1,0:T(8,128)(2,1)S(1)} collective-permute-done((bf16[128,512]{1,0:T(8,128)(2,1)S(1)}, bf16[128,512]{1,0:T(8,128)(2,1)S(1)}, u32[]{:S(2)}, u32[]{:S(2)}) %collective-permute-start) | collective-permute-done | bytes 131104 | tf_op jit(solution)/shard_map/ppermute | solution.py:41
  18.2 3.9 %collective-permute-start.4 = (bf16[128,512]{1,0:T(8,128)(2,1)S(1)}, bf16[128,512]{1,0:T(8,128)(2,1)S(1)}, u32[]{:S(2)}, u32[]{:S(2)}) collective-permute-start(bf16[128,512]{1,0:T(8,128)(2,1)S(1)} %collective-permute-done.1), channel_id=1, source_target_pairs={{0,14},{1,15},{2,0},{3,1},{4,2},{5,3},{6,4},{7,5},{8,6},{9,7},{10,... | collective-permute-start | bytes 393224 | tf_op jit(solution)/shard_map/ppermute | solution.py:41
  25.1 2.3 %collective-permute-start.7 = (bf16[2,256,512]{2,1,0:T(8,128)(2,1)S(1)}, bf16[2,256,512]{2,1,0:T(8,128)(2,1)S(1)}, u32[]{:S(2)}, u32[]{:S(2)}) collective-permute-start(bf16[2,256,512]{2,1,0:T(8,128)(2,1)S(1)} %shard_map.163), channel_id=1, source_target_pairs={{0,1},{1,0},{2,3},{3,2},{4,5},{5,4},{6,7},{7,6},{8,9},{9,8},{10,11... | collective-permute-start | bytes 1572872 | tf_op jit(solution)/shard_map/ppermute | solution.py:41
  28.3 2.4 %collective-permute-start.9 = (bf16[128,1536]{1,0:T(8,128)(2,1)S(1)}, bf16[128,1536]{1,0:T(8,128)(2,1)S(1)}, u32[]{:S(2)}, u32[]{:S(2)}) collective-permute-start(bf16[128,1536]{1,0:T(8,128)(2,1)S(1)} %get-tuple-element.93), channel_id=1, source_target_pairs={{0,14},{1,15},{2,0},{3,1},{4,2},{5,3},{6,4},{7,5},{8,6},{9,7},{10,... | collective-permute-start | bytes 1179656 | tf_op jit(solution)/shard_map/ppermute | solution.py:41
  33.9 3.2 %collective-permute-start.6 = (bf16[128,512]{1,0:T(8,128)(2,1)S(1)}, bf16[128,512]{1,0:T(8,128)(2,1)S(1)}, u32[]{:S(2)}, u32[]{:S(2)}) collective-permute-start(bf16[128,512]{1,0:T(8,128)(2,1)S(1)} %collective-permute-done.4), channel_id=1, source_target_pairs={{0,14},{1,15},{2,0},{3,1},{4,2},{5,3},{6,4},{7,5},{8,6},{9,7},{10,... | collective-permute-start | bytes 393224 | tf_op jit(solution)/shard_map/ppermute | solution.py:41
  37.1 3.2 %collective-permute-done.5 = bf16[128,512]{1,0:T(8,128)(2,1)S(1)} collective-permute-done((bf16[128,512]{1,0:T(8,128)(2,1)S(1)}, bf16[128,512]{1,0:T(8,128)(2,1)S(1)}, u32[]{:S(2)}, u32[]{:S(2)}) %collective-permute-start.5) | collective-permute-done | bytes 131104 | tf_op jit(solution)/shard_map/ppermute | solution.py:41
  40.3 2.5 %collective-permute-start.10 = (bf16[64,512]{1,0:T(8,128)(2,1)S(1)}, bf16[64,512]{1,0:T(8,128)(2,1)S(1)}, u32[]{:S(2)}, u32[]{:S(2)}) collective-permute-start(bf16[64,512]{1,0:T(8,128)(2,1)S(1)} %slice.10), channel_id=1, source_target_pairs={{0,2},{1,3},{2,4},{3,5},{4,6},{5,7},{6,8},{7,9},{8,10},{9,11},{10,... | collective-permute-start | bytes 196616 | tf_op jit(solution)/shard_map/ppermute | solution.py:41
  48.7 1.8 %collective-permute-start.13 = (bf16[1024,512]{1,0:T(8,128)(2,1)S(1)}, bf16[1024,512]{1,0:T(8,128)(2,1)S(1)}, u32[]{:S(2)}, u32[]{:S(2)}) collective-permute-start(bf16[1024,512]{1,0:T(8,128)(2,1)S(1)} %constant_dynamic-update-slice_fusion.near), channel_id=1, source_target_pairs={{0,48},{1,49},{2,50},{3,51},{4,52},{5,53},{6,54},{7,55},{8,56},{9,... | collective-permute-start | bytes 3145736 | tf_op jit(solution)/shard_map/ppermute | solution.py:41
  51.7 1.7 %collective-permute-start.21 = (bf16[256,1536]{1,0:T(8,128)(2,1)S(1)}, bf16[256,1536]{1,0:T(8,128)(2,1)S(1)}, u32[]{:S(2)}, u32[]{:S(2)}) collective-permute-start(bf16[256,1536]{1,0:T(8,128)(2,1)S(1)} %shard_map.165), channel_id=1, source_target_pairs={{0,2},{1,3},{2,4},{3,5},{4,6},{5,7},{6,8},{7,9},{8,10},{9,11},{10,... | collective-permute-start | bytes 2359304 | tf_op jit(solution)/shard_map/ppermute | solution.py:41
  54.9 14.3 %collective-permute-done.12.near = bf16[1024,512]{1,0:T(8,128)(2,1)S(1)} collective-permute-done((bf16[1024,512]{1,0:T(8,128)(2,1)S(1)}, bf16[1024,512]{1,0:T(8,128)(2,1)S(1)}, u32[]{:S(2)}, u32[]{:S(2)}) %collective-permute-start.12) | collective-permute-done | bytes 1048608 | tf_op jit(solution)/shard_map/ppermute | solution.py:41
  70.5 5.8 %collective-permute-done.14.twin = bf16[1024,512]{1,0:T(8,128)(2,1)S(1)} collective-permute-done((bf16[1024,512]{1,0:T(8,128)(2,1)S(1)}, bf16[1024,512]{1,0:T(8,128)(2,1)S(1)}, u32[]{:S(2)}, u32[]{:S(2)}) %collective-permute-start.14) | collective-permute-done | bytes 1048608 | tf_op jit(solution)/shard_map/ppermute | solution.py:41
  76.4 3.1 %collective-permute-start.17 = (bf16[1024,512]{1,0:T(8,128)(2,1)S(1)}, bf16[1024,512]{1,0:T(8,128)(2,1)S(1)}, u32[]{:S(2)}, u32[]{:S(2)}) collective-permute-start(bf16[1024,512]{1,0:T(8,128)(2,1)S(1)} %collective-permute-done.14.twin), channel_id=1, source_target_pairs={{0,48},{1,49},{2,50},{3,51},{4,52},{5,53},{6,54},{7,55},{8,56},{9,... | collective-permute-start | bytes 3145736 | tf_op jit(solution)/shard_map/ppermute | solution.py:41
  79.5 3.9 %collective-permute-done.20.refs_5_ = bf16[2,256,512]{2,1,0:T(8,128)(2,1)S(1)} collective-permute-done((bf16[2,256,512]{2,1,0:T(8,128)(2,1)S(1)}, bf16[2,256,512]{2,1,0:T(8,128)(2,1)S(1)}, u32[]{:S(2)}, u32[]{:S(2)}) %collective-permute-start.20) | collective-permute-done | bytes 524320 | tf_op jit(solution)/shard_map/ppermute | solution.py:41
  86.8 2.0 %collective-permute-start.23 = (bf16[256,1536]{1,0:T(8,128)(2,1)S(1)}, bf16[256,1536]{1,0:T(8,128)(2,1)S(1)}, u32[]{:S(2)}, u32[]{:S(2)}) collective-permute-start(bf16[256,1536]{1,0:T(8,128)(2,1)S(1)} %shard_map.168), channel_id=1, source_target_pairs={{0,2},{1,3},{2,4},{3,5},{4,6},{5,7},{6,8},{7,9},{8,10},{9,11},{10,... | collective-permute-start | bytes 2359304 | tf_op jit(solution)/shard_map/ppermute | solution.py:41
  90.1 2.9 %shard_map.172 = (f32[256,512]{1,0:T(8,128)S(1)}, bf16[256,8192]{1,0:T(8,128)(2,1)}) custom-call(s32[4]{0:T(128)S(1)} %pad_add_fusion.at, bf16[256,8192]{1,0:T(8,128)(2,1)S(1)} %bitcast.48, bf16[256,512]{1,0:T(8,128)(2,1)S(1)} %bitcast.62, bf16[1024,512]{1,0:T(8,128)(2,1)S(1)} %constant_dynamic-update-slice_fusion.near, ...), custom_call_target="tpu_custom_call" | custom-call | flops 1073741824 | bytes 6291456 | tf_op jit(solution)/shard_map/pallas_call | solution.py:71
  93.0 7.4 %collective-permute-done.19.refs_5_.came = bf16[3,256,512]{2,1,0:T(8,128)(2,1)S(1)} collective-permute-done((bf16[3,256,512]{2,1,0:T(8,128)(2,1)S(1)}, bf16[3,256,512]{2,1,0:T(8,128)(2,1)S(1)}, u32[]{:S(2)}, u32[]{:S(2)}) %collective-permute-start.19) | collective-permute-done | bytes 786464 | tf_op jit(solution)/shard_map/ppermute | solution.py:41
  100.5 3.0 %collective-permute-done.23.refs_6_ = bf16[256,1536]{1,0:T(8,128)(2,1)S(1)} collective-permute-done((bf16[256,1536]{1,0:T(8,128)(2,1)S(1)}, bf16[256,1536]{1,0:T(8,128)(2,1)S(1)}, u32[]{:S(2)}, u32[]{:S(2)}) %collective-permute-start.23) | collective-permute-done | bytes 786464 | tf_op jit(solution)/shard_map/ppermute | solution.py:41
  107.0 1.8 %collective-permute-start.26 = (bf16[256,1536]{1,0:T(8,128)(2,1)S(1)}, bf16[256,1536]{1,0:T(8,128)(2,1)S(1)}, u32[]{:S(2)}, u32[]{:S(2)}) collective-permute-start(bf16[256,1536]{1,0:T(8,128)(2,1)S(1)} %shard_map.171), channel_id=1, source_target_pairs={{0,14},{1,15},{2,0},{3,1},{4,2},{5,3},{6,4},{7,5},{8,6},{9,7},{10,... | collective-permute-start | bytes 2359304 | tf_op jit(solution)/shard_map/ppermute | solution.py:41
  109.1 3.0 %collective-permute-start.18 = (bf16[1024,512]{1,0:T(8,128)(2,1)S(1)}, bf16[1024,512]{1,0:T(8,128)(2,1)S(1)}, u32[]{:S(2)}, u32[]{:S(2)}) collective-permute-start(bf16[1024,512]{1,0:T(8,128)(2,1)S(1)} %collective-permute-done.17.twin), channel_id=1, source_target_pairs={{0,48},{1,49},{2,50},{3,51},{4,52},{5,53},{6,54},{7,55},{8,56},{9,... | collective-permute-start | bytes 3145736 | tf_op jit(solution)/shard_map/ppermute | solution.py:41
  112.1 3.0 %shard_map.173 = (f32[256,512]{1,0:T(8,128)S(1)}, bf16[256,8192]{1,0:T(8,128)(2,1)}) custom-call(s32[4]{0:T(128)S(1)} %pad_add_fusion.at, bf16[256,8192]{1,0:T(8,128)(2,1)S(1)} %bitcast.57, bf16[256,512]{1,0:T(8,128)(2,1)S(1)} %bitcast.63, bf16[1024,512]{1,0:T(8,128)(2,1)S(1)} %collective-permute-done.13.near, ...), custom_call_target="tpu_custom_call", output_to_operand_aliasing={{1}: (6, {})} | custom-call | flops 1073741824 | bytes 6291456 | tf_op jit(solution)/shard_map/pallas_call | solution.py:71
  115.0 3.0 %shard_map.174 = (f32[256,512]{1,0:T(8,128)S(1)}, bf16[256,8192]{1,0:T(8,128)(2,1)}) custom-call(s32[4]{0:T(128)S(1)} %pad_add_fusion.at, bf16[256,8192]{1,0:T(8,128)(2,1)S(1)} %bitcast.58, bf16[256,512]{1,0:T(8,128)(2,1)S(1)} %bitcast.64, bf16[1024,512]{1,0:T(8,128)(2,1)S(1)} %collective-permute-done.12.near, ...), custom_call_target="tpu_custom_call", output_to_operand_aliasing={{1}: (6, {})} | custom-call | flops 1073741824 | bytes 6291456 | tf_op jit(solution)/shard_map/pallas_call | solution.py:71
  118.0 3.3 %collective-permute-done.25.refs_0_.refs_2_ = bf16[256,1536]{1,0:T(8,128)(2,1)S(1)} collective-permute-done((bf16[256,1536]{1,0:T(8,128)(2,1)S(1)}, bf16[256,1536]{1,0:T(8,128)(2,1)S(1)}, u32[]{:S(2)}, u32[]{:S(2)}) %collective-permute-start.25) | collective-permute-done | bytes 786464 | tf_op jit(solution)/shard_map/ppermute | solution.py:41
  121.3 2.3 %shard_map.176 = (f32[256,384]{1,0:T(8,128)S(1)}, bf16[256,384]{1,0:T(8,128)(2,1)S(1)}, bf16[256,384]{1,0:T(8,128)(2,1)S(1)}, bf16[256,384]{1,0:T(8,128)(2,1)S(1)}) custom-call(s32[4]{0:T(128)S(1)} %pad_add_fusion.at, bf16[256,8192]{1,0:T(8,128)(2,1)S(1)} %bitcast.59, bf16[512,256]{1,0:T(8,128)(2,1)S(1)} %get-tuple-element.84.refs_4_.rows, ...), custom_call_target="tpu_custom_call" | custom-call | flops 201326592 | bytes 4194304 | tf_op jit(solution)/shard_map/pallas_call | solution.py:71
  124.0 2.7 %collective-permute-start.28 = (bf16[256,384]{1,0:T(8,128)(2,1)S(1)}, bf16[256,384]{1,0:T(8,128)(2,1)S(1)}, u32[]{:S(2)}, u32[]{:S(2)}) collective-permute-start(bf16[256,384]{1,0:T(8,128)(2,1)S(1)} %get-tuple-element.137), channel_id=1, source_target_pairs={{0,32},{1,33},{2,34},{3,35},{4,36},{5,37},{6,38},{7,39},{8,40},{9,... | collective-permute-start | bytes 589832 | tf_op jit(solution)/shard_map/ppermute | solution.py:41
  128.1 9.8 %collective-permute-done.27.in_1 = bf16[256,384]{1,0:T(8,128)(2,1)S(1)} collective-permute-done((bf16[256,384]{1,0:T(8,128)(2,1)S(1)}, bf16[256,384]{1,0:T(8,128)(2,1)S(1)}, u32[]{:S(2)}, u32[]{:S(2)}) %collective-permute-start.27) | collective-permute-done | bytes 196640 | tf_op jit(solution)/shard_map/ppermute | solution.py:41
  138.9 2.9 %collective-permute-start.30 = (bf16[256,128]{1,0:T(8,128)(2,1)S(1)}, bf16[256,128]{1,0:T(8,128)(2,1)S(1)}, u32[]{:S(2)}, u32[]{:S(2)}) collective-permute-start(bf16[256,128]{1,0:T(8,128)(2,1)S(1)} %get-tuple-element.143), channel_id=1, source_target_pairs={{0,1},{1,0},{2,3},{3,2},{4,5},{5,4},{6,7},{7,6},{8,9},{9,8},{10,11... | collective-permute-start | bytes 196616 | tf_op jit(solution)/shard_map/ppermute | solution.py:41
  142.2 2.6 %collective-permute-done.30.came = bf16[256,128]{1,0:T(8,128)(2,1)S(1)} collective-permute-done((bf16[256,128]{1,0:T(8,128)(2,1)S(1)}, bf16[256,128]{1,0:T(8,128)(2,1)S(1)}, u32[]{:S(2)}, u32[]{:S(2)}) %collective-permute-start.30) | collective-permute-done | bytes 65568 | tf_op jit(solution)/shard_map/ppermute | solution.py:41
  146.5 3.0 %shard_map.175 = (bf16[256,512]{1,0:T(8,128)(2,1)}, bf16[256,8192]{1,0:T(8,128)(2,1)}) custom-call(s32[4]{0:T(128)S(1)} %pad_add_fusion.at, bf16[256,8192]{1,0:T(8,128)(2,1)S(1)} %bitcast.60, bf16[256,512]{1,0:T(8,128)(2,1)S(1)} %bitcast.65, bf16[1024,512]{1,0:T(8,128)(2,1)S(1)} %collective-permute-done.15.near, ...), custom_call_target="tpu_custom_call", output_to_operand_aliasing={{1}: (6, {})} | custom-call | flops 1073741824 | bytes 6291456 | tf_op jit(solution)/shard_map/pallas_call | solution.py:71
  (91 shorter events, 33.5 us)
Async XLA Ops:
  6.6 11.5 %collective-permute-start.2 = (bf16[1,256,512]{2,1,0:T(8,128)(2,1)S(1)}, bf16[1,256,512]{2,1,0:T(8,128)(2,1)S(1)}, u32[]{:S(2)}, u32[]{:S(2)}) collective-permute-start(bf16[1,256,512]{2,1,0:T(8,128)(2,1)S(1)} %get-tuple-element.81), channel_id=1, source_target_pairs={{0,1},{1,0},{2,3},{3,2},{4,5},{5,4},{6,7},{7,6},{8,9},{9,8},{10,11... | collective-permute-start | bytes 786440 | tf_op jit(solution)/shard_map/ppermute | solution.py:41
  9.0 9.1 %collective-permute-start = (bf16[128,512]{1,0:T(8,128)(2,1)S(1)}, bf16[128,512]{1,0:T(8,128)(2,1)S(1)}, u32[]{:S(2)}, u32[]{:S(2)}) collective-permute-start(bf16[128,512]{1,0:T(8,128)(2,1)S(1)} %bitcast.66), channel_id=1, source_target_pairs={{0,2},{1,3},{2,4},{3,5},{4,6},{5,7},{6,8},{7,9},{8,10},{9,11},{10,... | collective-permute-start | bytes 393224 | tf_op jit(solution)/shard_map/ppermute | solution.py:41
  10.9 7.1 %collective-permute-start.1 = (bf16[128,512]{1,0:T(8,128)(2,1)S(1)}, bf16[128,512]{1,0:T(8,128)(2,1)S(1)}, u32[]{:S(2)}, u32[]{:S(2)}) collective-permute-start(bf16[128,512]{1,0:T(8,128)(2,1)S(1)} %bitcast.67), channel_id=1, source_target_pairs={{0,14},{1,15},{2,0},{3,1},{4,2},{5,3},{6,4},{7,5},{8,6},{9,7},{10,... | collective-permute-start | bytes 393224 | tf_op jit(solution)/shard_map/ppermute | solution.py:41
  18.1 7.0 %collective-permute-start.3 = (bf16[128,512]{1,0:T(8,128)(2,1)S(1)}, bf16[128,512]{1,0:T(8,128)(2,1)S(1)}, u32[]{:S(2)}, u32[]{:S(2)}) collective-permute-start(bf16[128,512]{1,0:T(8,128)(2,1)S(1)} %collective-permute-done), channel_id=1, source_target_pairs={{0,2},{1,3},{2,4},{3,5},{4,6},{5,7},{6,8},{7,9},{8,10},{9,11},{10,... | collective-permute-start | bytes 393224 | tf_op jit(solution)/shard_map/ppermute | solution.py:41
  18.2 6.9 %collective-permute-start.4 = (bf16[128,512]{1,0:T(8,128)(2,1)S(1)}, bf16[128,512]{1,0:T(8,128)(2,1)S(1)}, u32[]{:S(2)}, u32[]{:S(2)}) collective-permute-start(bf16[128,512]{1,0:T(8,128)(2,1)S(1)} %collective-permute-done.1), channel_id=1, source_target_pairs={{0,14},{1,15},{2,0},{3,1},{4,2},{5,3},{6,4},{7,5},{8,6},{9,7},{10,... | collective-permute-start | bytes 393224 | tf_op jit(solution)/shard_map/ppermute | solution.py:41
  25.1 18.6 %collective-permute-start.7 = (bf16[2,256,512]{2,1,0:T(8,128)(2,1)S(1)}, bf16[2,256,512]{2,1,0:T(8,128)(2,1)S(1)}, u32[]{:S(2)}, u32[]{:S(2)}) collective-permute-start(bf16[2,256,512]{2,1,0:T(8,128)(2,1)S(1)} %shard_map.163), channel_id=1, source_target_pairs={{0,1},{1,0},{2,3},{3,2},{4,5},{5,4},{6,7},{7,6},{8,9},{9,8},{10,11... | collective-permute-start | bytes 1572872 | tf_op jit(solution)/shard_map/ppermute | solution.py:41
  27.4 16.3 %collective-permute-start.8 = (bf16[128,1536]{1,0:T(8,128)(2,1)S(1)}, bf16[128,1536]{1,0:T(8,128)(2,1)S(1)}, u32[]{:S(2)}, u32[]{:S(2)}) collective-permute-start(bf16[128,1536]{1,0:T(8,128)(2,1)S(1)} %get-tuple-element.92), channel_id=1, source_target_pairs={{0,2},{1,3},{2,4},{3,5},{4,6},{5,7},{6,8},{7,9},{8,10},{9,11},{10,... | collective-permute-start | bytes 1179656 | tf_op jit(solution)/shard_map/ppermute | solution.py:41
  28.3 16.4 %collective-permute-start.9 = (bf16[128,1536]{1,0:T(8,128)(2,1)S(1)}, bf16[128,1536]{1,0:T(8,128)(2,1)S(1)}, u32[]{:S(2)}, u32[]{:S(2)}) collective-permute-start(bf16[128,1536]{1,0:T(8,128)(2,1)S(1)} %get-tuple-element.93), channel_id=1, source_target_pairs={{0,14},{1,15},{2,0},{3,1},{4,2},{5,3},{6,4},{7,5},{8,6},{9,7},{10,... | collective-permute-start | bytes 1179656 | tf_op jit(solution)/shard_map/ppermute | solution.py:41
  33.8 6.5 %collective-permute-start.5 = (bf16[128,512]{1,0:T(8,128)(2,1)S(1)}, bf16[128,512]{1,0:T(8,128)(2,1)S(1)}, u32[]{:S(2)}, u32[]{:S(2)}) collective-permute-start(bf16[128,512]{1,0:T(8,128)(2,1)S(1)} %collective-permute-done.3), channel_id=1, source_target_pairs={{0,2},{1,3},{2,4},{3,5},{4,6},{5,7},{6,8},{7,9},{8,10},{9,11},{10,... | collective-permute-start | bytes 393224 | tf_op jit(solution)/shard_map/ppermute | solution.py:41
  33.9 6.4 %collective-permute-start.6 = (bf16[128,512]{1,0:T(8,128)(2,1)S(1)}, bf16[128,512]{1,0:T(8,128)(2,1)S(1)}, u32[]{:S(2)}, u32[]{:S(2)}) collective-permute-start(bf16[128,512]{1,0:T(8,128)(2,1)S(1)} %collective-permute-done.4), channel_id=1, source_target_pairs={{0,14},{1,15},{2,0},{3,1},{4,2},{5,3},{6,4},{7,5},{8,6},{9,7},{10,... | collective-permute-start | bytes 393224 | tf_op jit(solution)/shard_map/ppermute | solution.py:41
  40.3 5.6 %collective-permute-start.10 = (bf16[64,512]{1,0:T(8,128)(2,1)S(1)}, bf16[64,512]{1,0:T(8,128)(2,1)S(1)}, u32[]{:S(2)}, u32[]{:S(2)}) collective-permute-start(bf16[64,512]{1,0:T(8,128)(2,1)S(1)} %slice.10), channel_id=1, source_target_pairs={{0,2},{1,3},{2,4},{3,5},{4,6},{5,7},{6,8},{7,9},{8,10},{9,11},{10,... | collective-permute-start | bytes 196616 | tf_op jit(solution)/shard_map/ppermute | solution.py:41
  42.8 4.3 %collective-permute-start.11 = (bf16[64,512]{1,0:T(8,128)(2,1)S(1)}, bf16[64,512]{1,0:T(8,128)(2,1)S(1)}, u32[]{:S(2)}, u32[]{:S(2)}) collective-permute-start(bf16[64,512]{1,0:T(8,128)(2,1)S(1)} %slice.11), channel_id=1, source_target_pairs={{0,14},{1,15},{2,0},{3,1},{4,2},{5,3},{6,4},{7,5},{8,6},{9,7},{10,... | collective-permute-start | bytes 196616 | tf_op jit(solution)/shard_map/ppermute | solution.py:41
  47.1 22.1 %collective-permute-start.12 = (bf16[1024,512]{1,0:T(8,128)(2,1)S(1)}, bf16[1024,512]{1,0:T(8,128)(2,1)S(1)}, u32[]{:S(2)}, u32[]{:S(2)}) collective-permute-start(bf16[1024,512]{1,0:T(8,128)(2,1)S(1)} %constant_dynamic-update-slice_fusion.near), channel_id=1, source_target_pairs={{0,16},{1,17},{2,18},{3,19},{4,20},{5,21},{6,22},{7,23},{8,24},{9,... | collective-permute-start | bytes 3145736 | tf_op jit(solution)/shard_map/ppermute | solution.py:41
  48.7 21.8 %collective-permute-start.13 = (bf16[1024,512]{1,0:T(8,128)(2,1)S(1)}, bf16[1024,512]{1,0:T(8,128)(2,1)S(1)}, u32[]{:S(2)}, u32[]{:S(2)}) collective-permute-start(bf16[1024,512]{1,0:T(8,128)(2,1)S(1)} %constant_dynamic-update-slice_fusion.near), channel_id=1, source_target_pairs={{0,48},{1,49},{2,50},{3,51},{4,52},{5,53},{6,54},{7,55},{8,56},{9,... | collective-permute-start | bytes 3145736 | tf_op jit(solution)/shard_map/ppermute | solution.py:41
  50.4 25.9 %collective-permute-start.14 = (bf16[1024,512]{1,0:T(8,128)(2,1)S(1)}, bf16[1024,512]{1,0:T(8,128)(2,1)S(1)}, u32[]{:S(2)}, u32[]{:S(2)}) collective-permute-start(bf16[1024,512]{1,0:T(8,128)(2,1)S(1)} %constant_dynamic-update-slice_fusion.near), channel_id=1, source_target_pairs={{0,1},{1,0},{2,3},{3,2},{4,5},{5,4},{6,7},{7,6},{8,9},{9,8},{10,11... | collective-permute-start | bytes 3145736 | tf_op jit(solution)/shard_map/ppermute | solution.py:41
  51.7 33.1 %collective-permute-start.21 = (bf16[256,1536]{1,0:T(8,128)(2,1)S(1)}, bf16[256,1536]{1,0:T(8,128)(2,1)S(1)}, u32[]{:S(2)}, u32[]{:S(2)}) collective-permute-start(bf16[256,1536]{1,0:T(8,128)(2,1)S(1)} %shard_map.165), channel_id=1, source_target_pairs={{0,2},{1,3},{2,4},{3,5},{4,6},{5,7},{6,8},{7,9},{8,10},{9,11},{10,... | collective-permute-start | bytes 2359304 | tf_op jit(solution)/shard_map/ppermute | solution.py:41
  53.4 32.4 %collective-permute-start.22 = (bf16[256,1536]{1,0:T(8,128)(2,1)S(1)}, bf16[256,1536]{1,0:T(8,128)(2,1)S(1)}, u32[]{:S(2)}, u32[]{:S(2)}) collective-permute-start(bf16[256,1536]{1,0:T(8,128)(2,1)S(1)} %shard_map.166), channel_id=1, source_target_pairs={{0,14},{1,15},{2,0},{3,1},{4,2},{5,3},{6,4},{7,5},{8,6},{9,7},{10,... | collective-permute-start | bytes 2359304 | tf_op jit(solution)/shard_map/ppermute | solution.py:41
  69.2 14.3 %collective-permute-start.20 = (bf16[2,256,512]{2,1,0:T(8,128)(2,1)S(1)}, bf16[2,256,512]{2,1,0:T(8,128)(2,1)S(1)}, u32[]{:S(2)}, u32[]{:S(2)}) collective-permute-start(bf16[2,256,512]{2,1,0:T(8,128)(2,1)S(1)} %shard_map.164), channel_id=1, source_target_pairs={{0,1},{1,0},{2,3},{3,2},{4,5},{5,4},{6,7},{7,6},{8,9},{9,8},{10,11... | collective-permute-start | bytes 1572872 | tf_op jit(solution)/shard_map/ppermute | solution.py:41
  76.3 32.8 %collective-permute-start.16 = (bf16[1024,512]{1,0:T(8,128)(2,1)S(1)}, bf16[1024,512]{1,0:T(8,128)(2,1)S(1)}, u32[]{:S(2)}, u32[]{:S(2)}) collective-permute-start(bf16[1024,512]{1,0:T(8,128)(2,1)S(1)} %collective-permute-done.14.twin), channel_id=1, source_target_pairs={{0,16},{1,17},{2,18},{3,19},{4,20},{5,21},{6,22},{7,23},{8,24},{9,... | collective-permute-start | bytes 3145736 | tf_op jit(solution)/shard_map/ppermute | solution.py:41
  76.4 32.6 %collective-permute-start.17 = (bf16[1024,512]{1,0:T(8,128)(2,1)S(1)}, bf16[1024,512]{1,0:T(8,128)(2,1)S(1)}, u32[]{:S(2)}, u32[]{:S(2)}) collective-permute-start(bf16[1024,512]{1,0:T(8,128)(2,1)S(1)} %collective-permute-done.14.twin), channel_id=1, source_target_pairs={{0,48},{1,49},{2,50},{3,51},{4,52},{5,53},{6,54},{7,55},{8,56},{9,... | collective-permute-start | bytes 3145736 | tf_op jit(solution)/shard_map/ppermute | solution.py:41
  83.5 17.0 %collective-permute-start.19 = (bf16[3,256,512]{2,1,0:T(8,128)(2,1)S(1)}, bf16[3,256,512]{2,1,0:T(8,128)(2,1)S(1)}, u32[]{:S(2)}, u32[]{:S(2)}) collective-permute-start(bf16[3,256,512]{2,1,0:T(8,128)(2,1)S(1)} %shard_map.167), channel_id=1, source_target_pairs={{0,1},{1,0},{2,3},{3,2},{4,5},{5,4},{6,7},{7,6},{8,9},{9,8},{10,11... | collective-permute-start | bytes 2359304 | tf_op jit(solution)/shard_map/ppermute | solution.py:41
  86.8 16.7 %collective-permute-start.23 = (bf16[256,1536]{1,0:T(8,128)(2,1)S(1)}, bf16[256,1536]{1,0:T(8,128)(2,1)S(1)}, u32[]{:S(2)}, u32[]{:S(2)}) collective-permute-start(bf16[256,1536]{1,0:T(8,128)(2,1)S(1)} %shard_map.168), channel_id=1, source_target_pairs={{0,2},{1,3},{2,4},{3,5},{4,6},{5,7},{6,8},{7,9},{8,10},{9,11},{10,... | collective-permute-start | bytes 2359304 | tf_op jit(solution)/shard_map/ppermute | solution.py:41
  88.8 15.6 %collective-permute-start.24 = (bf16[256,1536]{1,0:T(8,128)(2,1)S(1)}, bf16[256,1536]{1,0:T(8,128)(2,1)S(1)}, u32[]{:S(2)}, u32[]{:S(2)}) collective-permute-start(bf16[256,1536]{1,0:T(8,128)(2,1)S(1)} %shard_map.169), channel_id=1, source_target_pairs={{0,14},{1,15},{2,0},{3,1},{4,2},{5,3},{6,4},{7,5},{8,6},{9,7},{10,... | collective-permute-start | bytes 2359304 | tf_op jit(solution)/shard_map/ppermute | solution.py:41
  105.5 15.7 %collective-permute-start.25 = (bf16[256,1536]{1,0:T(8,128)(2,1)S(1)}, bf16[256,1536]{1,0:T(8,128)(2,1)S(1)}, u32[]{:S(2)}, u32[]{:S(2)}) collective-permute-start(bf16[256,1536]{1,0:T(8,128)(2,1)S(1)} %shard_map.170), channel_id=1, source_target_pairs={{0,2},{1,3},{2,4},{3,5},{4,6},{5,7},{6,8},{7,9},{8,10},{9,11},{10,... | collective-permute-start | bytes 2359304 | tf_op jit(solution)/shard_map/ppermute | solution.py:41
  107.0 14.3 %collective-permute-start.26 = (bf16[256,1536]{1,0:T(8,128)(2,1)S(1)}, bf16[256,1536]{1,0:T(8,128)(2,1)S(1)}, u32[]{:S(2)}, u32[]{:S(2)}) collective-permute-start(bf16[256,1536]{1,0:T(8,128)(2,1)S(1)} %shard_map.171), channel_id=1, source_target_pairs={{0,14},{1,15},{2,0},{3,1},{4,2},{5,3},{6,4},{7,5},{8,6},{9,7},{10,... | collective-permute-start | bytes 2359304 | tf_op jit(solution)/shard_map/ppermute | solution.py:41
  108.8 37.7 %collective-permute-start.15 = (bf16[1024,512]{1,0:T(8,128)(2,1)S(1)}, bf16[1024,512]{1,0:T(8,128)(2,1)S(1)}, u32[]{:S(2)}, u32[]{:S(2)}) collective-permute-start(bf16[1024,512]{1,0:T(8,128)(2,1)S(1)} %collective-permute-done.12.near), channel_id=1, source_target_pairs={{0,16},{1,17},{2,18},{3,19},{4,20},{5,21},{6,22},{7,23},{8,24},{9,... | collective-permute-start | bytes 3145736 | tf_op jit(solution)/shard_map/ppermute | solution.py:41
  109.1 37.4 %collective-permute-start.18 = (bf16[1024,512]{1,0:T(8,128)(2,1)S(1)}, bf16[1024,512]{1,0:T(8,128)(2,1)S(1)}, u32[]{:S(2)}, u32[]{:S(2)}) collective-permute-start(bf16[1024,512]{1,0:T(8,128)(2,1)S(1)} %collective-permute-done.17.twin), channel_id=1, source_target_pairs={{0,48},{1,49},{2,50},{3,51},{4,52},{5,53},{6,54},{7,55},{8,56},{9,... | collective-permute-start | bytes 3145736 | tf_op jit(solution)/shard_map/ppermute | solution.py:41
  112.0 14.7 %collective-permute-start.31 = (bf16[128,128]{1,0:T(8,128)(2,1)S(1)}, bf16[128,128]{1,0:T(8,128)(2,1)S(1)}, u32[]{:S(2)}, u32[]{:S(2)}) collective-permute-start(bf16[128,128]{1,0:T(8,128)(2,1)S(1)} %bitcast.70), channel_id=1, source_target_pairs={{0,64},{1,65},{2,66},{3,67},{4,68},{5,69},{6,70},{7,71},{8,72},{9,... | collective-permute-start | bytes 98312 | tf_op jit(solution)/shard_map/ppermute | solution.py:41
  123.5 14.4 %collective-permute-start.27 = (bf16[256,384]{1,0:T(8,128)(2,1)S(1)}, bf16[256,384]{1,0:T(8,128)(2,1)S(1)}, u32[]{:S(2)}, u32[]{:S(2)}) collective-permute-start(bf16[256,384]{1,0:T(8,128)(2,1)S(1)} %get-tuple-element.136), channel_id=1, source_target_pairs={{0,16},{1,17},{2,18},{3,19},{4,20},{5,21},{6,22},{7,23},{8,24},{9,... | collective-permute-start | bytes 589832 | tf_op jit(solution)/shard_map/ppermute | solution.py:41
  124.0 14.3 %collective-permute-start.28 = (bf16[256,384]{1,0:T(8,128)(2,1)S(1)}, bf16[256,384]{1,0:T(8,128)(2,1)S(1)}, u32[]{:S(2)}, u32[]{:S(2)}) collective-permute-start(bf16[256,384]{1,0:T(8,128)(2,1)S(1)} %get-tuple-element.137), channel_id=1, source_target_pairs={{0,32},{1,33},{2,34},{3,35},{4,36},{5,37},{6,38},{7,39},{8,40},{9,... | collective-permute-start | bytes 589832 | tf_op jit(solution)/shard_map/ppermute | solution.py:41
  126.7 11.5 %collective-permute-start.29 = (bf16[256,384]{1,0:T(8,128)(2,1)S(1)}, bf16[256,384]{1,0:T(8,128)(2,1)S(1)}, u32[]{:S(2)}, u32[]{:S(2)}) collective-permute-start(bf16[256,384]{1,0:T(8,128)(2,1)S(1)} %get-tuple-element.138), channel_id=1, source_target_pairs={{0,48},{1,49},{2,50},{3,51},{4,52},{5,53},{6,54},{7,55},{8,56},{9,... | collective-permute-start | bytes 589832 | tf_op jit(solution)/shard_map/ppermute | solution.py:41
  138.9 5.9 %collective-permute-start.30 = (bf16[256,128]{1,0:T(8,128)(2,1)S(1)}, bf16[256,128]{1,0:T(8,128)(2,1)S(1)}, u32[]{:S(2)}, u32[]{:S(2)}) collective-permute-start(bf16[256,128]{1,0:T(8,128)(2,1)S(1)} %get-tuple-element.143), channel_id=1, source_target_pairs={{0,1},{1,0},{2,3},{3,2},{4,5},{5,4},{6,7},{7,6},{8,9},{9,8},{10,11... | collective-permute-start | bytes 196616 | tf_op jit(solution)/shard_map/ppermute | solution.py:41
  (13 other events, 166.2 us)

commit v2 on v1

--- a/solution.py
+++ b/solution.py
@@ -354,8 +354,10 @@
     own, *pieces = last_block(tokens, rows, twin_4, 2, right, left, at)
     came = spread_x(pieces)
     keep, send = split_y(own, came, at)
+    keep, send, *state = together(keep, send, *state)
     came = moved(send, dy=2)
     state = use_weight(tokens, cotangent, (near_far, twin_far), state, at, 2, True)
+    keep, came, state = together(keep, came, state)
     return state, (keep, came)
 
 

time: 151 us -> 145 us (0.960)
  waiting for transfers between devices: 59.1 us -> 51 us
    ppermute x32, waiting for transfers between devices: 58.6 us -> 51 us  [moved(): return lax.ppermute(value, AXES, sorted(pairs))]
  transfers between devices with their start and end apart: 33 -> 33, of which waited for: 14 -> 13; matrix products, arithmetic and copies ran while one was open for 0% -> 0% of each run, Pallas kernels for 17% -> 18%
where the time goes in v2:
time: 145 us; the launch traced here: 142 us
  starting transfers between devices  56.4 us (39%)
  waiting for transfers between devices  51 us (35%)
  Pallas kernels  28.6 us (20%)
  local copies, waits for them, and re-layouts  4.48 us (3%)
  between operations  1.67 us (1%)
    ppermute x32, starting transfers between devices, moved(): return lax.ppermute(value, AXES, sorted(pairs))  55.1 us
    ppermute x32, waiting for transfers between devices, moved(): return lax.ppermute(value, AXES, sorted(pairs))  51 us
    pallas_call x18, Pallas kernels, call(): pl.pallas_call(kernel, out_shape=shapes, grid_spec=pltpu.PrefetchScalarGr...  28.6 us
    unnamed x32, local copies, waits for them, and re-layouts  3.87 us
  transfers between devices with their start and end apart: 33, of which 13 were waited for; matrix products, arithmetic and copies ran while one was open for 0% of the time, Pallas kernels for 18%

profile of v2, /device:TPU:8, one launch (start us, length us, event | category | flops | bytes accessed | tf_op | source)
XLA Modules:
  0.0 142.2 jit_solution(1867163148038020557)
XLA Ops:
  2.6 2.2 %copy-done.1 = bf16[1,256,8192]{2,1,0:T(8,128)(2,1)S(1)} copy-done((bf16[1,256,8192]{2,1,0:T(8,128)(2,1)S(1)}, bf16[1,256,8192]{2,1,0:T(8,128)(2,1)}, u32[]{:S(2)}) %copy-start.1) | copy-done | bytes 4194328
  6.6 2.4 %collective-permute-start.2 = (bf16[1,256,512]{2,1,0:T(8,128)(2,1)S(1)}, bf16[1,256,512]{2,1,0:T(8,128)(2,1)S(1)}, u32[]{:S(2)}, u32[]{:S(2)}) collective-permute-start(bf16[1,256,512]{2,1,0:T(8,128)(2,1)S(1)} %get-tuple-element.90), channel_id=1, source_target_pairs={{0,1},{1,0},{2,3},{3,2},{4,5},{5,4},{6,7},{7,6},{8,9},{9,8},{10,11... | collective-permute-start | bytes 786440 | tf_op jit(solution)/shard_map/ppermute | solution.py:41
  9.0 1.9 %collective-permute-start = (bf16[128,512]{1,0:T(8,128)(2,1)S(1)}, bf16[128,512]{1,0:T(8,128)(2,1)S(1)}, u32[]{:S(2)}, u32[]{:S(2)}) collective-permute-start(bf16[128,512]{1,0:T(8,128)(2,1)S(1)} %bitcast.66), channel_id=1, source_target_pairs={{0,2},{1,3},{2,4},{3,5},{4,6},{5,7},{6,8},{7,9},{8,10},{9,11},{10,... | collective-permute-start | bytes 393224 | tf_op jit(solution)/shard_map/ppermute | solution.py:41
  10.9 3.9 %collective-permute-start.1 = (bf16[128,512]{1,0:T(8,128)(2,1)S(1)}, bf16[128,512]{1,0:T(8,128)(2,1)S(1)}, u32[]{:S(2)}, u32[]{:S(2)}) collective-permute-start(bf16[128,512]{1,0:T(8,128)(2,1)S(1)} %bitcast.67), channel_id=1, source_target_pairs={{0,14},{1,15},{2,0},{3,1},{4,2},{5,3},{6,4},{7,5},{8,6},{9,7},{10,... | collective-permute-start | bytes 393224 | tf_op jit(solution)/shard_map/ppermute | solution.py:41
  14.9 3.2 %collective-permute-done = bf16[128,512]{1,0:T(8,128)(2,1)S(1)} collective-permute-done((bf16[128,512]{1,0:T(8,128)(2,1)S(1)}, bf16[128,512]{1,0:T(8,128)(2,1)S(1)}, u32[]{:S(2)}, u32[]{:S(2)}) %collective-permute-start) | collective-permute-done | bytes 131104 | tf_op jit(solution)/shard_map/ppermute | solution.py:41
  18.2 3.9 %collective-permute-start.4 = (bf16[128,512]{1,0:T(8,128)(2,1)S(1)}, bf16[128,512]{1,0:T(8,128)(2,1)S(1)}, u32[]{:S(2)}, u32[]{:S(2)}) collective-permute-start(bf16[128,512]{1,0:T(8,128)(2,1)S(1)} %collective-permute-done.1), channel_id=1, source_target_pairs={{0,14},{1,15},{2,0},{3,1},{4,2},{5,3},{6,4},{7,5},{8,6},{9,7},{10,... | collective-permute-start | bytes 393224 | tf_op jit(solution)/shard_map/ppermute | solution.py:41
  25.1 2.3 %collective-permute-start.7 = (bf16[2,256,512]{2,1,0:T(8,128)(2,1)S(1)}, bf16[2,256,512]{2,1,0:T(8,128)(2,1)S(1)}, u32[]{:S(2)}, u32[]{:S(2)}) collective-permute-start(bf16[2,256,512]{2,1,0:T(8,128)(2,1)S(1)} %shard_map.163), channel_id=1, source_target_pairs={{0,1},{1,0},{2,3},{3,2},{4,5},{5,4},{6,7},{7,6},{8,9},{9,8},{10,11... | collective-permute-start | bytes 1572872 | tf_op jit(solution)/shard_map/ppermute | solution.py:41
  28.3 2.4 %collective-permute-start.9 = (bf16[128,1536]{1,0:T(8,128)(2,1)S(1)}, bf16[128,1536]{1,0:T(8,128)(2,1)S(1)}, u32[]{:S(2)}, u32[]{:S(2)}) collective-permute-start(bf16[128,1536]{1,0:T(8,128)(2,1)S(1)} %get-tuple-element.101), channel_id=1, source_target_pairs={{0,14},{1,15},{2,0},{3,1},{4,2},{5,3},{6,4},{7,5},{8,6},{9,7},{10,... | collective-permute-start | bytes 1179656 | tf_op jit(solution)/shard_map/ppermute | solution.py:41
  32.0 1.7 %shard_map.167 = bf16[3,256,512]{2,1,0:T(8,128)(2,1)S(1)} custom-call(s32[4]{0:T(128)S(1)} %pad_add_fusion.at, bf16[256,8192]{1,0:T(8,128)(2,1)S(1)} %bitcast.28, bf16[256,8192]{1,0:T(8,128)(2,1)S(1)} %bitcast.29, bf16[256,8192]{1,0:T(8,128)(2,1)S(1)} %bitcast.30, bf16[256,8192]{1,0:T(8,128)(2,1)S(1)} %bitcast.31, bf16[256,256]{1,0:T(8,128)(2,1)S(1)} %slice.9.refs_4_), custom_call_target="tpu_custom_call" | custom-call | flops 201326592 | bytes 1572864 | tf_op jit(solution)/shard_map/pallas_call | solution.py:71
  33.9 3.2 %collective-permute-start.6 = (bf16[128,512]{1,0:T(8,128)(2,1)S(1)}, bf16[128,512]{1,0:T(8,128)(2,1)S(1)}, u32[]{:S(2)}, u32[]{:S(2)}) collective-permute-start(bf16[128,512]{1,0:T(8,128)(2,1)S(1)} %collective-permute-done.4), channel_id=1, source_target_pairs={{0,14},{1,15},{2,0},{3,1},{4,2},{5,3},{6,4},{7,5},{8,6},{9,7},{10,... | collective-permute-start | bytes 393224 | tf_op jit(solution)/shard_map/ppermute | solution.py:41
  37.1 3.2 %collective-permute-done.5 = bf16[128,512]{1,0:T(8,128)(2,1)S(1)} collective-permute-done((bf16[128,512]{1,0:T(8,128)(2,1)S(1)}, bf16[128,512]{1,0:T(8,128)(2,1)S(1)}, u32[]{:S(2)}, u32[]{:S(2)}) %collective-permute-start.5) | collective-permute-done | bytes 131104 | tf_op jit(solution)/shard_map/ppermute | solution.py:41
  40.3 2.5 %collective-permute-start.10 = (bf16[64,512]{1,0:T(8,128)(2,1)S(1)}, bf16[64,512]{1,0:T(8,128)(2,1)S(1)}, u32[]{:S(2)}, u32[]{:S(2)}) collective-permute-start(bf16[64,512]{1,0:T(8,128)(2,1)S(1)} %slice.10), channel_id=1, source_target_pairs={{0,2},{1,3},{2,4},{3,5},{4,6},{5,7},{6,8},{7,9},{8,10},{9,11},{10,... | collective-permute-start | bytes 196616 | tf_op jit(solution)/shard_map/ppermute | solution.py:41
  48.7 1.8 %collective-permute-start.19 = (bf16[1024,512]{1,0:T(8,128)(2,1)S(1)}, bf16[1024,512]{1,0:T(8,128)(2,1)S(1)}, u32[]{:S(2)}, u32[]{:S(2)}) collective-permute-start(bf16[1024,512]{1,0:T(8,128)(2,1)S(1)} %constant_dynamic-update-slice_fusion.near), channel_id=1, source_target_pairs={{0,48},{1,49},{2,50},{3,51},{4,52},{5,53},{6,54},{7,55},{8,56},{9,... | collective-permute-start | bytes 3145736 | tf_op jit(solution)/shard_map/ppermute | solution.py:41
  51.7 1.7 %collective-permute-start.14 = (bf16[256,1536]{1,0:T(8,128)(2,1)S(1)}, bf16[256,1536]{1,0:T(8,128)(2,1)S(1)}, u32[]{:S(2)}, u32[]{:S(2)}) collective-permute-start(bf16[256,1536]{1,0:T(8,128)(2,1)S(1)} %shard_map.165), channel_id=1, source_target_pairs={{0,2},{1,3},{2,4},{3,5},{4,6},{5,7},{6,8},{7,9},{8,10},{9,11},{10,... | collective-permute-start | bytes 2359304 | tf_op jit(solution)/shard_map/ppermute | solution.py:41
  54.9 14.3 %collective-permute-done.18.near = bf16[1024,512]{1,0:T(8,128)(2,1)S(1)} collective-permute-done((bf16[1024,512]{1,0:T(8,128)(2,1)S(1)}, bf16[1024,512]{1,0:T(8,128)(2,1)S(1)}, u32[]{:S(2)}, u32[]{:S(2)}) %collective-permute-start.18) | collective-permute-done | bytes 1048608 | tf_op jit(solution)/shard_map/ppermute | solution.py:41
  70.5 5.8 %collective-permute-done.20.twin = bf16[1024,512]{1,0:T(8,128)(2,1)S(1)} collective-permute-done((bf16[1024,512]{1,0:T(8,128)(2,1)S(1)}, bf16[1024,512]{1,0:T(8,128)(2,1)S(1)}, u32[]{:S(2)}, u32[]{:S(2)}) %collective-permute-start.20) | collective-permute-done | bytes 1048608 | tf_op jit(solution)/shard_map/ppermute | solution.py:41
  76.5 3.1 %collective-permute-start.24 = (bf16[1024,512]{1,0:T(8,128)(2,1)S(1)}, bf16[1024,512]{1,0:T(8,128)(2,1)S(1)}, u32[]{:S(2)}, u32[]{:S(2)}) collective-permute-start(bf16[1024,512]{1,0:T(8,128)(2,1)S(1)} %collective-permute-done.20.twin), channel_id=1, source_target_pairs={{0,48},{1,49},{2,50},{3,51},{4,52},{5,53},{6,54},{7,55},{8,56},{9,... | collective-permute-start | bytes 3145736 | tf_op jit(solution)/shard_map/ppermute | solution.py:41
  79.5 4.0 %collective-permute-done.13.refs_5_ = bf16[2,256,512]{2,1,0:T(8,128)(2,1)S(1)} collective-permute-done((bf16[2,256,512]{2,1,0:T(8,128)(2,1)S(1)}, bf16[2,256,512]{2,1,0:T(8,128)(2,1)S(1)}, u32[]{:S(2)}, u32[]{:S(2)}) %collective-permute-start.13) | collective-permute-done | bytes 524320 | tf_op jit(solution)/shard_map/ppermute | solution.py:41
  86.8 2.0 %collective-permute-start.16 = (bf16[256,1536]{1,0:T(8,128)(2,1)S(1)}, bf16[256,1536]{1,0:T(8,128)(2,1)S(1)}, u32[]{:S(2)}, u32[]{:S(2)}) collective-permute-start(bf16[256,1536]{1,0:T(8,128)(2,1)S(1)} %shard_map.168), channel_id=1, source_target_pairs={{0,2},{1,3},{2,4},{3,5},{4,6},{5,7},{6,8},{7,9},{8,10},{9,11},{10,... | collective-permute-start | bytes 2359304 | tf_op jit(solution)/shard_map/ppermute | solution.py:41
  90.1 6.2 %collective-permute-done.23.twin = bf16[1024,512]{1,0:T(8,128)(2,1)S(1)} collective-permute-done((bf16[1024,512]{1,0:T(8,128)(2,1)S(1)}, bf16[1024,512]{1,0:T(8,128)(2,1)S(1)}, u32[]{:S(2)}, u32[]{:S(2)}) %collective-permute-start.23) | collective-permute-done | bytes 1048608 | tf_op jit(solution)/shard_map/ppermute | solution.py:41
  96.3 3.2 %collective-permute-start.30 = (bf16[1024,512]{1,0:T(8,128)(2,1)S(1)}, bf16[1024,512]{1,0:T(8,128)(2,1)S(1)}, u32[]{:S(2)}, u32[]{:S(2)}) collective-permute-start(bf16[1024,512]{1,0:T(8,128)(2,1)S(1)} %collective-permute-done.24.twin), channel_id=1, source_target_pairs={{0,48},{1,49},{2,50},{3,51},{4,52},{5,53},{6,54},{7,55},{8,56},{9,... | collective-permute-start | bytes 3145736 | tf_op jit(solution)/shard_map/ppermute | solution.py:41
  99.5 2.9 %shard_map.172 = (f32[256,512]{1,0:T(8,128)S(1)}, bf16[256,8192]{1,0:T(8,128)(2,1)}) custom-call(s32[4]{0:T(128)S(1)} %pad_add_fusion.at, bf16[256,8192]{1,0:T(8,128)(2,1)S(1)} %bitcast.48, bf16[256,512]{1,0:T(8,128)(2,1)S(1)} %bitcast.62, bf16[1024,512]{1,0:T(8,128)(2,1)S(1)} %constant_dynamic-update-slice_fusion.near, ...), custom_call_target="tpu_custom_call" | custom-call | flops 1073741824 | bytes 6291456 | tf_op jit(solution)/shard_map/pallas_call | solution.py:71
  105.5 2.8 %collective-permute-start.21 = (bf16[256,1536]{1,0:T(8,128)(2,1)S(1)}, bf16[256,1536]{1,0:T(8,128)(2,1)S(1)}, u32[]{:S(2)}, u32[]{:S(2)}) collective-permute-start(bf16[256,1536]{1,0:T(8,128)(2,1)S(1)} %shard_map.170), channel_id=1, source_target_pairs={{0,2},{1,3},{2,4},{3,5},{4,6},{5,7},{6,8},{7,9},{8,10},{9,11},{10,... | collective-permute-start | bytes 2359304 | tf_op jit(solution)/shard_map/ppermute | solution.py:41
  109.5 3.0 %shard_map.173 = (f32[256,512]{1,0:T(8,128)S(1)}, bf16[256,8192]{1,0:T(8,128)(2,1)}) custom-call(s32[4]{0:T(128)S(1)} %pad_add_fusion.at, bf16[256,8192]{1,0:T(8,128)(2,1)S(1)} %bitcast.57, bf16[256,512]{1,0:T(8,128)(2,1)S(1)} %bitcast.63, bf16[1024,512]{1,0:T(8,128)(2,1)S(1)} %collective-permute-done.19.near, ...), custom_call_target="tpu_custom_call", output_to_operand_aliasing={{1}: (6, {})} | custom-call | flops 1073741824 | bytes 6291456 | tf_op jit(solution)/shard_map/pallas_call | solution.py:71
  112.4 3.0 %shard_map.174 = (f32[256,512]{1,0:T(8,128)S(1)}, bf16[256,8192]{1,0:T(8,128)(2,1)}) custom-call(s32[4]{0:T(128)S(1)} %pad_add_fusion.at, bf16[256,8192]{1,0:T(8,128)(2,1)S(1)} %bitcast.58, bf16[256,512]{1,0:T(8,128)(2,1)S(1)} %bitcast.64, bf16[1024,512]{1,0:T(8,128)(2,1)S(1)} %collective-permute-done.18.near, ...), custom_call_target="tpu_custom_call", output_to_operand_aliasing={{1}: (6, {})} | custom-call | flops 1073741824 | bytes 6291456 | tf_op jit(solution)/shard_map/pallas_call | solution.py:71
  115.4 5.9 %collective-permute-done.21.refs_0_.refs_2_ = bf16[256,1536]{1,0:T(8,128)(2,1)S(1)} collective-permute-done((bf16[256,1536]{1,0:T(8,128)(2,1)S(1)}, bf16[256,1536]{1,0:T(8,128)(2,1)S(1)}, u32[]{:S(2)}, u32[]{:S(2)}) %collective-permute-start.21) | collective-permute-done | bytes 786464 | tf_op jit(solution)/shard_map/ppermute | solution.py:41
  121.3 2.2 %shard_map.175 = (f32[256,384]{1,0:T(8,128)S(1)}, bf16[256,384]{1,0:T(8,128)(2,1)S(1)}, bf16[256,384]{1,0:T(8,128)(2,1)S(1)}, bf16[256,384]{1,0:T(8,128)(2,1)S(1)}) custom-call(s32[4]{0:T(128)S(1)} %pad_add_fusion.at, bf16[256,8192]{1,0:T(8,128)(2,1)S(1)} %bitcast.59, bf16[512,256]{1,0:T(8,128)(2,1)S(1)} %get-tuple-element.87.refs_4_.rows, ...), custom_call_target="tpu_custom_call" | custom-call | flops 201326592 | bytes 4194304 | tf_op jit(solution)/shard_map/pallas_call | solution.py:71
  123.9 2.7 %collective-permute-start.26 = (bf16[256,384]{1,0:T(8,128)(2,1)S(1)}, bf16[256,384]{1,0:T(8,128)(2,1)S(1)}, u32[]{:S(2)}, u32[]{:S(2)}) collective-permute-start(bf16[256,384]{1,0:T(8,128)(2,1)S(1)} %get-tuple-element.141), channel_id=1, source_target_pairs={{0,32},{1,33},{2,34},{3,35},{4,36},{5,37},{6,38},{7,39},{8,40},{9,... | collective-permute-start | bytes 589832 | tf_op jit(solution)/shard_map/ppermute | solution.py:41
  128.1 4.5 %collective-permute-done.25.in_1 = bf16[256,384]{1,0:T(8,128)(2,1)S(1)} collective-permute-done((bf16[256,384]{1,0:T(8,128)(2,1)S(1)}, bf16[256,384]{1,0:T(8,128)(2,1)S(1)}, u32[]{:S(2)}, u32[]{:S(2)}) %collective-permute-start.25) | collective-permute-done | bytes 196640 | tf_op jit(solution)/shard_map/ppermute | solution.py:41
  134.6 2.0 %collective-permute-start.28 = (bf16[256,128]{1,0:T(8,128)(2,1)S(1)}, bf16[256,128]{1,0:T(8,128)(2,1)S(1)}, u32[]{:S(2)}, u32[]{:S(2)}) collective-permute-start(bf16[256,128]{1,0:T(8,128)(2,1)S(1)} %get-tuple-element.151), channel_id=1, source_target_pairs={{0,1},{1,0},{2,3},{3,2},{4,5},{5,4},{6,7},{7,6},{8,9},{9,8},{10,11... | collective-permute-start | bytes 196616 | tf_op jit(solution)/shard_map/ppermute | solution.py:41
  136.6 3.0 %shard_map.177 = (bf16[256,512]{1,0:T(8,128)(2,1)}, bf16[256,8192]{1,0:T(8,128)(2,1)}) custom-call(s32[4]{0:T(128)S(1)} %pad_add_fusion.at, bf16[256,8192]{1,0:T(8,128)(2,1)S(1)} %bitcast.60, bf16[256,512]{1,0:T(8,128)(2,1)S(1)} %bitcast.65, bf16[1024,512]{1,0:T(8,128)(2,1)S(1)} %collective-permute-done.29.near, ...), custom_call_target="tpu_custom_call", output_to_operand_aliasing={{1}: (6, {})} | custom-call | flops 1073741824 | bytes 6291456 | tf_op jit(solution)/shard_map/pallas_call | solution.py:71
  140.5 1.7 %shard_map.178 = (bf16[1,128,512]{2,1,0:T(8,128)(2,1)}, bf16[1,128,512]{2,1,0:T(8,128)(2,1)}, bf16[1,128,512]{2,1,0:T(8,128)(2,1)}, f32[128,128]{1,0:T(8,128)}, ...) custom-call(s32[4]{0:T(128)S(1)} %copy-done.10, f32[512,128]{1,0:T(8,128)S(1)} %get-tuple-element.158.keep, ...), custom_call_target="tpu_custom_call" | custom-call | flops 2097152 | bytes 3145728 | tf_op jit(solution)/shard_map/pallas_call | solution.py:71
  (91 shorter events, 31.8 us)
Async XLA Ops:
  6.6 11.5 %collective-permute-start.2 = (bf16[1,256,512]{2,1,0:T(8,128)(2,1)S(1)}, bf16[1,256,512]{2,1,0:T(8,128)(2,1)S(1)}, u32[]{:S(2)}, u32[]{:S(2)}) collective-permute-start(bf16[1,256,512]{2,1,0:T(8,128)(2,1)S(1)} %get-tuple-element.90), channel_id=1, source_target_pairs={{0,1},{1,0},{2,3},{3,2},{4,5},{5,4},{6,7},{7,6},{8,9},{9,8},{10,11... | collective-permute-start | bytes 786440 | tf_op jit(solution)/shard_map/ppermute | solution.py:41
  9.0 9.1 %collective-permute-start = (bf16[128,512]{1,0:T(8,128)(2,1)S(1)}, bf16[128,512]{1,0:T(8,128)(2,1)S(1)}, u32[]{:S(2)}, u32[]{:S(2)}) collective-permute-start(bf16[128,512]{1,0:T(8,128)(2,1)S(1)} %bitcast.66), channel_id=1, source_target_pairs={{0,2},{1,3},{2,4},{3,5},{4,6},{5,7},{6,8},{7,9},{8,10},{9,11},{10,... | collective-permute-start | bytes 393224 | tf_op jit(solution)/shard_map/ppermute | solution.py:41
  10.9 7.1 %collective-permute-start.1 = (bf16[128,512]{1,0:T(8,128)(2,1)S(1)}, bf16[128,512]{1,0:T(8,128)(2,1)S(1)}, u32[]{:S(2)}, u32[]{:S(2)}) collective-permute-start(bf16[128,512]{1,0:T(8,128)(2,1)S(1)} %bitcast.67), channel_id=1, source_target_pairs={{0,14},{1,15},{2,0},{3,1},{4,2},{5,3},{6,4},{7,5},{8,6},{9,7},{10,... | collective-permute-start | bytes 393224 | tf_op jit(solution)/shard_map/ppermute | solution.py:41
  18.1 7.0 %collective-permute-start.3 = (bf16[128,512]{1,0:T(8,128)(2,1)S(1)}, bf16[128,512]{1,0:T(8,128)(2,1)S(1)}, u32[]{:S(2)}, u32[]{:S(2)}) collective-permute-start(bf16[128,512]{1,0:T(8,128)(2,1)S(1)} %collective-permute-done), channel_id=1, source_target_pairs={{0,2},{1,3},{2,4},{3,5},{4,6},{5,7},{6,8},{7,9},{8,10},{9,11},{10,... | collective-permute-start | bytes 393224 | tf_op jit(solution)/shard_map/ppermute | solution.py:41
  18.2 6.9 %collective-permute-start.4 = (bf16[128,512]{1,0:T(8,128)(2,1)S(1)}, bf16[128,512]{1,0:T(8,128)(2,1)S(1)}, u32[]{:S(2)}, u32[]{:S(2)}) collective-permute-start(bf16[128,512]{1,0:T(8,128)(2,1)S(1)} %collective-permute-done.1), channel_id=1, source_target_pairs={{0,14},{1,15},{2,0},{3,1},{4,2},{5,3},{6,4},{7,5},{8,6},{9,7},{10,... | collective-permute-start | bytes 393224 | tf_op jit(solution)/shard_map/ppermute | solution.py:41
  25.1 18.6 %collective-permute-start.7 = (bf16[2,256,512]{2,1,0:T(8,128)(2,1)S(1)}, bf16[2,256,512]{2,1,0:T(8,128)(2,1)S(1)}, u32[]{:S(2)}, u32[]{:S(2)}) collective-permute-start(bf16[2,256,512]{2,1,0:T(8,128)(2,1)S(1)} %shard_map.163), channel_id=1, source_target_pairs={{0,1},{1,0},{2,3},{3,2},{4,5},{5,4},{6,7},{7,6},{8,9},{9,8},{10,11... | collective-permute-start | bytes 1572872 | tf_op jit(solution)/shard_map/ppermute | solution.py:41
  27.4 16.3 %collective-permute-start.8 = (bf16[128,1536]{1,0:T(8,128)(2,1)S(1)}, bf16[128,1536]{1,0:T(8,128)(2,1)S(1)}, u32[]{:S(2)}, u32[]{:S(2)}) collective-permute-start(bf16[128,1536]{1,0:T(8,128)(2,1)S(1)} %get-tuple-element.100), channel_id=1, source_target_pairs={{0,2},{1,3},{2,4},{3,5},{4,6},{5,7},{6,8},{7,9},{8,10},{9,11},{10,... | collective-permute-start | bytes 1179656 | tf_op jit(solution)/shard_map/ppermute | solution.py:41
  28.3 16.4 %collective-permute-start.9 = (bf16[128,1536]{1,0:T(8,128)(2,1)S(1)}, bf16[128,1536]{1,0:T(8,128)(2,1)S(1)}, u32[]{:S(2)}, u32[]{:S(2)}) collective-permute-start(bf16[128,1536]{1,0:T(8,128)(2,1)S(1)} %get-tuple-element.101), channel_id=1, source_target_pairs={{0,14},{1,15},{2,0},{3,1},{4,2},{5,3},{6,4},{7,5},{8,6},{9,7},{10,... | collective-permute-start | bytes 1179656 | tf_op jit(solution)/shard_map/ppermute | solution.py:41
  33.8 6.5 %collective-permute-start.5 = (bf16[128,512]{1,0:T(8,128)(2,1)S(1)}, bf16[128,512]{1,0:T(8,128)(2,1)S(1)}, u32[]{:S(2)}, u32[]{:S(2)}) collective-permute-start(bf16[128,512]{1,0:T(8,128)(2,1)S(1)} %collective-permute-done.3), channel_id=1, source_target_pairs={{0,2},{1,3},{2,4},{3,5},{4,6},{5,7},{6,8},{7,9},{8,10},{9,11},{10,... | collective-permute-start | bytes 393224 | tf_op jit(solution)/shard_map/ppermute | solution.py:41
  33.9 6.4 %collective-permute-start.6 = (bf16[128,512]{1,0:T(8,128)(2,1)S(1)}, bf16[128,512]{1,0:T(8,128)(2,1)S(1)}, u32[]{:S(2)}, u32[]{:S(2)}) collective-permute-start(bf16[128,512]{1,0:T(8,128)(2,1)S(1)} %collective-permute-done.4), channel_id=1, source_target_pairs={{0,14},{1,15},{2,0},{3,1},{4,2},{5,3},{6,4},{7,5},{8,6},{9,7},{10,... | collective-permute-start | bytes 393224 | tf_op jit(solution)/shard_map/ppermute | solution.py:41
  40.3 5.6 %collective-permute-start.10 = (bf16[64,512]{1,0:T(8,128)(2,1)S(1)}, bf16[64,512]{1,0:T(8,128)(2,1)S(1)}, u32[]{:S(2)}, u32[]{:S(2)}) collective-permute-start(bf16[64,512]{1,0:T(8,128)(2,1)S(1)} %slice.10), channel_id=1, source_target_pairs={{0,2},{1,3},{2,4},{3,5},{4,6},{5,7},{6,8},{7,9},{8,10},{9,11},{10,... | collective-permute-start | bytes 196616 | tf_op jit(solution)/shard_map/ppermute | solution.py:41
  47.1 22.1 %collective-permute-start.18 = (bf16[1024,512]{1,0:T(8,128)(2,1)S(1)}, bf16[1024,512]{1,0:T(8,128)(2,1)S(1)}, u32[]{:S(2)}, u32[]{:S(2)}) collective-permute-start(bf16[1024,512]{1,0:T(8,128)(2,1)S(1)} %constant_dynamic-update-slice_fusion.near), channel_id=1, source_target_pairs={{0,16},{1,17},{2,18},{3,19},{4,20},{5,21},{6,22},{7,23},{8,24},{9,... | collective-permute-start | bytes 3145736 | tf_op jit(solution)/shard_map/ppermute | solution.py:41
  48.7 21.8 %collective-permute-start.19 = (bf16[1024,512]{1,0:T(8,128)(2,1)S(1)}, bf16[1024,512]{1,0:T(8,128)(2,1)S(1)}, u32[]{:S(2)}, u32[]{:S(2)}) collective-permute-start(bf16[1024,512]{1,0:T(8,128)(2,1)S(1)} %constant_dynamic-update-slice_fusion.near), channel_id=1, source_target_pairs={{0,48},{1,49},{2,50},{3,51},{4,52},{5,53},{6,54},{7,55},{8,56},{9,... | collective-permute-start | bytes 3145736 | tf_op jit(solution)/shard_map/ppermute | solution.py:41
  50.4 25.9 %collective-permute-start.20 = (bf16[1024,512]{1,0:T(8,128)(2,1)S(1)}, bf16[1024,512]{1,0:T(8,128)(2,1)S(1)}, u32[]{:S(2)}, u32[]{:S(2)}) collective-permute-start(bf16[1024,512]{1,0:T(8,128)(2,1)S(1)} %constant_dynamic-update-slice_fusion.near), channel_id=1, source_target_pairs={{0,1},{1,0},{2,3},{3,2},{4,5},{5,4},{6,7},{7,6},{8,9},{9,8},{10,11... | collective-permute-start | bytes 3145736 | tf_op jit(solution)/shard_map/ppermute | solution.py:41
  51.7 33.1 %collective-permute-start.14 = (bf16[256,1536]{1,0:T(8,128)(2,1)S(1)}, bf16[256,1536]{1,0:T(8,128)(2,1)S(1)}, u32[]{:S(2)}, u32[]{:S(2)}) collective-permute-start(bf16[256,1536]{1,0:T(8,128)(2,1)S(1)} %shard_map.165), channel_id=1, source_target_pairs={{0,2},{1,3},{2,4},{3,5},{4,6},{5,7},{6,8},{7,9},{8,10},{9,11},{10,... | collective-permute-start | bytes 2359304 | tf_op jit(solution)/shard_map/ppermute | solution.py:41
  53.4 32.4 %collective-permute-start.15 = (bf16[256,1536]{1,0:T(8,128)(2,1)S(1)}, bf16[256,1536]{1,0:T(8,128)(2,1)S(1)}, u32[]{:S(2)}, u32[]{:S(2)}) collective-permute-start(bf16[256,1536]{1,0:T(8,128)(2,1)S(1)} %shard_map.166), channel_id=1, source_target_pairs={{0,14},{1,15},{2,0},{3,1},{4,2},{5,3},{6,4},{7,5},{8,6},{9,7},{10,... | collective-permute-start | bytes 2359304 | tf_op jit(solution)/shard_map/ppermute | solution.py:41
  69.2 14.3 %collective-permute-start.13 = (bf16[2,256,512]{2,1,0:T(8,128)(2,1)S(1)}, bf16[2,256,512]{2,1,0:T(8,128)(2,1)S(1)}, u32[]{:S(2)}, u32[]{:S(2)}) collective-permute-start(bf16[2,256,512]{2,1,0:T(8,128)(2,1)S(1)} %shard_map.164), channel_id=1, source_target_pairs={{0,1},{1,0},{2,3},{3,2},{4,5},{5,4},{6,7},{7,6},{8,9},{9,8},{10,11... | collective-permute-start | bytes 1572872 | tf_op jit(solution)/shard_map/ppermute | solution.py:41
  76.3 20.0 %collective-permute-start.23 = (bf16[1024,512]{1,0:T(8,128)(2,1)S(1)}, bf16[1024,512]{1,0:T(8,128)(2,1)S(1)}, u32[]{:S(2)}, u32[]{:S(2)}) collective-permute-start(bf16[1024,512]{1,0:T(8,128)(2,1)S(1)} %collective-permute-done.20.twin), channel_id=1, source_target_pairs={{0,16},{1,17},{2,18},{3,19},{4,20},{5,21},{6,22},{7,23},{8,24},{9,... | collective-permute-start | bytes 3145736 | tf_op jit(solution)/shard_map/ppermute | solution.py:41
  76.5 19.8 %collective-permute-start.24 = (bf16[1024,512]{1,0:T(8,128)(2,1)S(1)}, bf16[1024,512]{1,0:T(8,128)(2,1)S(1)}, u32[]{:S(2)}, u32[]{:S(2)}) collective-permute-start(bf16[1024,512]{1,0:T(8,128)(2,1)S(1)} %collective-permute-done.20.twin), channel_id=1, source_target_pairs={{0,48},{1,49},{2,50},{3,51},{4,52},{5,53},{6,54},{7,55},{8,56},{9,... | collective-permute-start | bytes 3145736 | tf_op jit(solution)/shard_map/ppermute | solution.py:41
  83.5 19.0 %collective-permute-start.12 = (bf16[3,256,512]{2,1,0:T(8,128)(2,1)S(1)}, bf16[3,256,512]{2,1,0:T(8,128)(2,1)S(1)}, u32[]{:S(2)}, u32[]{:S(2)}) collective-permute-start(bf16[3,256,512]{2,1,0:T(8,128)(2,1)S(1)} %shard_map.167), channel_id=1, source_target_pairs={{0,1},{1,0},{2,3},{3,2},{4,5},{5,4},{6,7},{7,6},{8,9},{9,8},{10,11... | collective-permute-start | bytes 2359304 | tf_op jit(solution)/shard_map/ppermute | solution.py:41
  86.8 16.7 %collective-permute-start.16 = (bf16[256,1536]{1,0:T(8,128)(2,1)S(1)}, bf16[256,1536]{1,0:T(8,128)(2,1)S(1)}, u32[]{:S(2)}, u32[]{:S(2)}) collective-permute-start(bf16[256,1536]{1,0:T(8,128)(2,1)S(1)} %shard_map.168), channel_id=1, source_target_pairs={{0,2},{1,3},{2,4},{3,5},{4,6},{5,7},{6,8},{7,9},{8,10},{9,11},{10,... | collective-permute-start | bytes 2359304 | tf_op jit(solution)/shard_map/ppermute | solution.py:41
  88.8 15.6 %collective-permute-start.17 = (bf16[256,1536]{1,0:T(8,128)(2,1)S(1)}, bf16[256,1536]{1,0:T(8,128)(2,1)S(1)}, u32[]{:S(2)}, u32[]{:S(2)}) collective-permute-start(bf16[256,1536]{1,0:T(8,128)(2,1)S(1)} %shard_map.169), channel_id=1, source_target_pairs={{0,14},{1,15},{2,0},{3,1},{4,2},{5,3},{6,4},{7,5},{8,6},{9,7},{10,... | collective-permute-start | bytes 2359304 | tf_op jit(solution)/shard_map/ppermute | solution.py:41
  96.3 40.3 %collective-permute-start.29 = (bf16[1024,512]{1,0:T(8,128)(2,1)S(1)}, bf16[1024,512]{1,0:T(8,128)(2,1)S(1)}, u32[]{:S(2)}, u32[]{:S(2)}) collective-permute-start(bf16[1024,512]{1,0:T(8,128)(2,1)S(1)} %collective-permute-done.18.near), channel_id=1, source_target_pairs={{0,16},{1,17},{2,18},{3,19},{4,20},{5,21},{6,22},{7,23},{8,24},{9,... | collective-permute-start | bytes 3145736 | tf_op jit(solution)/shard_map/ppermute | solution.py:41
  96.3 40.3 %collective-permute-start.30 = (bf16[1024,512]{1,0:T(8,128)(2,1)S(1)}, bf16[1024,512]{1,0:T(8,128)(2,1)S(1)}, u32[]{:S(2)}, u32[]{:S(2)}) collective-permute-start(bf16[1024,512]{1,0:T(8,128)(2,1)S(1)} %collective-permute-done.24.twin), channel_id=1, source_target_pairs={{0,48},{1,49},{2,50},{3,51},{4,52},{5,53},{6,54},{7,55},{8,56},{9,... | collective-permute-start | bytes 3145736 | tf_op jit(solution)/shard_map/ppermute | solution.py:41
  105.5 15.7 %collective-permute-start.21 = (bf16[256,1536]{1,0:T(8,128)(2,1)S(1)}, bf16[256,1536]{1,0:T(8,128)(2,1)S(1)}, u32[]{:S(2)}, u32[]{:S(2)}) collective-permute-start(bf16[256,1536]{1,0:T(8,128)(2,1)S(1)} %shard_map.170), channel_id=1, source_target_pairs={{0,2},{1,3},{2,4},{3,5},{4,6},{5,7},{6,8},{7,9},{8,10},{9,11},{10,... | collective-permute-start | bytes 2359304 | tf_op jit(solution)/shard_map/ppermute | solution.py:41
  108.3 12.9 %collective-permute-start.22 = (bf16[256,1536]{1,0:T(8,128)(2,1)S(1)}, bf16[256,1536]{1,0:T(8,128)(2,1)S(1)}, u32[]{:S(2)}, u32[]{:S(2)}) collective-permute-start(bf16[256,1536]{1,0:T(8,128)(2,1)S(1)} %shard_map.171), channel_id=1, source_target_pairs={{0,14},{1,15},{2,0},{3,1},{4,2},{5,3},{6,4},{7,5},{8,6},{9,7},{10,... | collective-permute-start | bytes 2359304 | tf_op jit(solution)/shard_map/ppermute | solution.py:41
  109.5 17.2 %collective-permute-start.31 = (bf16[128,128]{1,0:T(8,128)(2,1)S(1)}, bf16[128,128]{1,0:T(8,128)(2,1)S(1)}, u32[]{:S(2)}, u32[]{:S(2)}) collective-permute-start(bf16[128,128]{1,0:T(8,128)(2,1)S(1)} %bitcast.70), channel_id=1, source_target_pairs={{0,64},{1,65},{2,66},{3,67},{4,68},{5,69},{6,70},{7,71},{8,72},{9,... | collective-permute-start | bytes 98312 | tf_op jit(solution)/shard_map/ppermute | solution.py:41
  123.5 9.1 %collective-permute-start.25 = (bf16[256,384]{1,0:T(8,128)(2,1)S(1)}, bf16[256,384]{1,0:T(8,128)(2,1)S(1)}, u32[]{:S(2)}, u32[]{:S(2)}) collective-permute-start(bf16[256,384]{1,0:T(8,128)(2,1)S(1)} %get-tuple-element.140), channel_id=1, source_target_pairs={{0,16},{1,17},{2,18},{3,19},{4,20},{5,21},{6,22},{7,23},{8,24},{9,... | collective-permute-start | bytes 589832 | tf_op jit(solution)/shard_map/ppermute | solution.py:41
  123.9 9.9 %collective-permute-start.26 = (bf16[256,384]{1,0:T(8,128)(2,1)S(1)}, bf16[256,384]{1,0:T(8,128)(2,1)S(1)}, u32[]{:S(2)}, u32[]{:S(2)}) collective-permute-start(bf16[256,384]{1,0:T(8,128)(2,1)S(1)} %get-tuple-element.141), channel_id=1, source_target_pairs={{0,32},{1,33},{2,34},{3,35},{4,36},{5,37},{6,38},{7,39},{8,40},{9,... | collective-permute-start | bytes 589832 | tf_op jit(solution)/shard_map/ppermute | solution.py:41
  126.7 7.2 %collective-permute-start.27 = (bf16[256,384]{1,0:T(8,128)(2,1)S(1)}, bf16[256,384]{1,0:T(8,128)(2,1)S(1)}, u32[]{:S(2)}, u32[]{:S(2)}) collective-permute-start(bf16[256,384]{1,0:T(8,128)(2,1)S(1)} %get-tuple-element.142), channel_id=1, source_target_pairs={{0,48},{1,49},{2,50},{3,51},{4,52},{5,53},{6,54},{7,55},{8,56},{9,... | collective-permute-start | bytes 589832 | tf_op jit(solution)/shard_map/ppermute | solution.py:41
  132.6 7.9 %collective-permute-start.32 = (bf16[2,128,128]{2,1,0:T(8,128)(2,1)S(1)}, bf16[2,128,128]{2,1,0:T(8,128)(2,1)S(1)}, u32[]{:S(2)}, u32[]{:S(2)}) collective-permute-start(bf16[2,128,128]{2,1,0:T(8,128)(2,1)S(1)} %pad_maximum_fusion.two), channel_id=1, source_target_pairs={{0,128},{1,129},{2,130},{3,131},{4,132},{5,133},{6,134},{7,135},{8... | collective-permute-start | bytes 196616 | tf_op jit(solution)/shard_map/ppermute | solution.py:49
  134.6 5.9 %collective-permute-start.28 = (bf16[256,128]{1,0:T(8,128)(2,1)S(1)}, bf16[256,128]{1,0:T(8,128)(2,1)S(1)}, u32[]{:S(2)}, u32[]{:S(2)}) collective-permute-start(bf16[256,128]{1,0:T(8,128)(2,1)S(1)} %get-tuple-element.151), channel_id=1, source_target_pairs={{0,1},{1,0},{2,3},{3,2},{4,5},{5,4},{6,7},{7,6},{8,9},{9,8},{10,11... | collective-permute-start | bytes 196616 | tf_op jit(solution)/shard_map/ppermute | solution.py:41
  (13 other events, 75.0 us)
